TPU v7x, 128 devices: a whole 4x4x4 slice. The times are simulated.
128 devices in a mesh: row: 8 (over x, z_lo), col: 16 (over z_hi, y, core).
Axes of the slice: x: 4, y: 4, z: 4 (z_hi: 2, z_lo: 2; z = z_hi * 2 + z_lo), core: 2. Of those that a mesh axis runs over, the one named last changes fastest.
Arguments:
- coarse_feat: bfloat16 [1536, 64, 512], P(('row', 'col')), may hold values from -6 to 6
- coarse_children: int32 [1536, 8], P(('row', 'col')), may hold values from -1 to 6143, as said below
- fine_neighbours: int32 [6144, 26], P(('row', 'col')), may hold values from -1 to 6143, as said below
- up_weight: bfloat16 [64, 864], replicated, may hold values from -0.375 to 0.375
- up_bias: float32 [32], replicated, may hold values from -3 to 3
- conv_weight: bfloat16 [32, 864], replicated, may hold values from -0.21875 to 0.21875
- conv_bias: float32 [32], replicated, may hold values from -3 to 3
Outputs:
- fine_features: bfloat16 [6144, 32, 512], P(('row', 'col'))
Inputs may be any that keep to these rules, and one draw needn't show every extreme that they name: `coarse_children`: entry [c, o] is the global index of the fine block that is octant o = 4 ox + 2 oy + oz of coarse block c, or -1 when that child is absent. The children present, taken in order of c and then o, are numbered 0, 1, 2 and so on without gaps, so every fine block has exactly one parent and every coarse block has one to seven children. The device holding a fine block is the device holding its parent or one of the two beside it in row-major order of the mesh. `fine_neighbours`: column j stands for direction j of the 26 directions (dx, dy, dz) in the finite set (-1, 0, 1)^3 other than (0, 0, 0) in lexicographic order. The relation is symmetric: if entry [b, j] is n then entry [n, 25 - j] is b. Entries in columns 13 to 25 are larger than b, those in columns 0 to 12 smaller, and every entry lies within 12 of b; so at most 12 blocks of one device have a neighbour on the device after it, and likewise before it.
All inputs are finite; a program needn't handle non-finite values.
Results may differ from a plain program's by a relative error of at most 0.0052.
Values may be sent and summed in bfloat16 or wider, within the bound.
A program may use at most 256 MiB of HBM per device.

v0:
```python
import jax
import jax.numpy as jnp
import numpy as np
from jax import lax
from jax.sharding import PartitionSpec as P

direction_list = [
    (code // 9 - 1, code // 3 % 3 - 1, code % 3 - 1) for code in range(27) if code != 13
]
upward_list = [(0, 0, 1), (0, 1, 0), (0, 1, 1), (1, 0, 0), (1, 0, 1), (1, 1, 0), (1, 1, 1)]
upward_columns = [
    9 * (delta[0] + 1) + 3 * (delta[1] + 1) + (delta[2] + 1) - 1 for delta in upward_list
]
spill_sizes = [8 ** sum((1 for component in delta if component == 0)) for delta in upward_list]
spill_starts = [sum(spill_sizes[:number]) for number in range(7)]
tap_shifts = [100 * (code // 9) + 10 * (code // 3 % 3) + code % 3 for code in range(27)]


def passed_along(block, axis, distance):
    devices = range(lax.axis_size(axis))
    route = [(i - distance, i) for i in devices if i - distance in devices]
    return lax.ppermute(block, axis, route)


def cells_of(fixed):
    free_axes = [which for which in range(3) if fixed[which] is None]
    listed = []
    for local in range(8 ** len(free_axes)):
        coords = [0 if value is None else value for value in fixed]
        remain = local
        for which in reversed(free_axes):
            coords[which] = remain % 8
            remain = remain // 8
        listed.append((local, coords))
    return listed


def cell_index(coords):
    return 64 * coords[0] + 8 * coords[1] + coords[2]


def octant_table():
    table = np.zeros((512, 512), np.float32)
    for octant in range(8):
        corner = (octant // 4, octant // 2 % 2, octant % 2)
        for voxel in range(64):
            inner = (voxel // 16, voxel // 4 % 4, voxel % 4)
            table[
                cell_index([4 * corner[which] + inner[which] for which in range(3)]),
                octant * 64 + voxel,
            ] = 1.0
    return table


def place_table():
    table = np.zeros((4, 3, 9), np.float32)
    for voxel in range(4):
        for tap in range(3):
            table[voxel, tap, 2 * voxel + tap] = 1.0
    return table


def spill_matrix():
    table = np.zeros((7, 256, 512), np.float32)
    for number, delta in enumerate(upward_list):
        fixed = [7 if component == 1 else None for component in delta]
        for local, coords in cells_of(fixed):
            table[number, spill_starts[number] + local, cell_index(coords)] = 1.0
    return table


def facet_matrix():
    table = np.zeros((512, 384), np.float32)
    fixed_list = [
        (0, None, None),
        (7, None, None),
        (None, 0, None),
        (None, 7, None),
        (None, None, 0),
        (None, None, 7),
    ]
    for sheet_no, fixed in enumerate(fixed_list):
        for local, coords in cells_of(fixed):
            table[cell_index(coords), sheet_no * 64 + local] = 1.0
    return table


def facet_choice():
    listed = []
    for delta in direction_list:
        which_axis = [number for number in range(3) if delta[number] != 0][0]
        listed.append(2 * which_axis + (0 if delta[which_axis] == 1 else 1))
    return listed


def right_product(values, table):
    return lax.dot_general(
        values, table, (((values.ndim - 1,), (0,)), ((), ())), preferred_element_type=jnp.float32
    )


def octant_blocks(coarse_feat):
    count, channels = (coarse_feat.shape[0], coarse_feat.shape[1])
    moved = right_product(coarse_feat, jnp.asarray(octant_table(), jnp.bfloat16)).astype(
        jnp.bfloat16
    )
    return jnp.transpose(moved.reshape(count, channels, 8, 64), (0, 2, 1, 3)).reshape(
        count * 8, channels, 64
    )


def upsample(blocks, up_weight):
    count = blocks.shape[0]
    cout = up_weight.shape[1] // 27
    tap_out = lax.dot_general(
        blocks, up_weight, (((1,), (0,)), ((), ())), preferred_element_type=jnp.float32
    )
    shaped = tap_out.reshape(count, 4, 4, 4, 3, 3, 3, cout)
    placer = jnp.asarray(place_table(), jnp.float32)
    highest = lax.Precision.HIGHEST
    first = jnp.einsum("bxyzuvwc,xui->bcyzvwi", shaped, placer, precision=highest)
    second = jnp.einsum("bcyzvwi,yvj->bcijzw", first, placer, precision=highest)
    grid = jnp.einsum("bcijzw,zwk->bcijk", second, placer, precision=highest)
    portions = [grid[:, :, 1:9, 1:9, 1:9].reshape(count, cout, 512)]
    for delta in upward_list:
        picks = tuple((slice(0, 1) if component == 1 else slice(1, 9) for component in delta))
        portions.append(grid[(slice(None), slice(None)) + picks].reshape(count, cout, -1))
    portions.append(jnp.zeros((count, cout, 39), jnp.float32))
    return jnp.concatenate(portions, axis=2).astype(jnp.bfloat16)


def finish_hidden(base, added, up_bias):
    total = base.astype(jnp.float32) + added + up_bias[None, :, None]
    return jax.nn.silu(total).astype(jnp.bfloat16)


def cube_of(hidden_part):
    count, cout = (hidden_part.shape[0], hidden_part.shape[1])
    cube = hidden_part.reshape(count, cout, 8, 8, 8)
    return jnp.pad(cube, ((0, 0), (0, 0), (1, 1), (1, 1), (1, 1)))


def flatten_cube(padded):
    count, cout = (padded.shape[0], padded.shape[1])
    return jnp.pad(padded.reshape(count, cout, 1000), ((0, 0), (0, 0), (0, 24)))


def place_sheets(hidden_part, chosen):
    count, cout = (hidden_part.shape[0], hidden_part.shape[1])
    padded = cube_of(hidden_part)
    for column, delta in enumerate(direction_list):
        which_axis = [number for number in range(3) if delta[number] != 0][0]
        sheet = chosen[:, column].reshape(count, cout, 8, 8)
        picks = tuple(
            (
                7 if delta[number] == -1 else 0 if delta[number] == 1 else slice(None)
                for number in range(3)
                if number != which_axis
            )
        )
        sheet = sheet[(slice(None), slice(None)) + picks]
        target = tuple(
            (0 if component == -1 else 9 if component == 1 else slice(1, 9) for component in delta)
        )
        padded = padded.at[(slice(None), slice(None)) + target].set(sheet)
    return flatten_cube(padded)


def conv_finish(padded, weight_taps, conv_bias):
    count, cout = (padded.shape[0], conv_bias.shape[0])
    spread = jnp.einsum(
        "oc,ncp->nop", weight_taps, padded, preferred_element_type=jnp.float32
    ).reshape(count, 27, cout, 1024)
    total = spread[:, 0, :, 0:800]
    for code in range(1, 27):
        shift_now = tap_shifts[code]
        total = total + spread[:, code, :, shift_now : shift_now + 800]
    total = (total + conv_bias[None, :, None]).astype(jnp.bfloat16)
    total = jnp.pad(total, ((0, 0), (0, 0), (0, 200))).reshape(count, cout, 10, 10, 10)
    return total[:, :, 0:8, 0:8, 0:8].reshape(count, cout, 512)


def on_device(
    coarse_feat, coarse_children, fine_neighbours, up_weight, up_bias, conv_weight, conv_bias
):
    fine_count = fine_neighbours.shape[0]
    cout = conv_weight.shape[0]
    rank_here = lax.axis_index(("row", "col"))
    own_start = rank_here * fine_count
    octants = octant_blocks(coarse_feat)
    children = coarse_children.reshape(-1)
    heading = jnp.where(children >= 0, children // fine_count - rank_here, 5)
    landing = jnp.where(children >= 0, children % fine_count, 0)

    def route(values, offset):
        slots = jnp.where(heading == offset, landing, fine_count)
        source = (
            jnp.zeros((fine_count,), jnp.int32)
            .at[slots]
            .set(jnp.arange(children.shape[0], dtype=jnp.int32), mode="drop")
        )
        filled = jnp.zeros((fine_count,), jnp.bool_).at[slots].set(True, mode="drop")
        return jnp.where(filled[:, None, None], values[source], jnp.zeros((), values.dtype))

    joined = upsample(octants, up_weight)
    combined = route(joined, 0)
    for offset in (1, -1):
        combined = combined + passed_along(route(joined, offset), ("row", "col"), offset)
    base = combined[:, :, :512]
    spill = combined[:, :, 512:]
    spill_np = spill_matrix()
    spill_parts = jnp.asarray(spill_np, jnp.bfloat16)
    relative = fine_neighbours - own_start
    upward = fine_neighbours[:, upward_columns]
    upward_rel = relative[:, upward_columns]
    spill_zero = jnp.zeros((1, cout, 256), jnp.bfloat16)
    spill_next = passed_along(spill, ("row", "col"), -1)
    spill_table = jnp.concatenate([spill, spill_next, spill_zero], axis=0)
    spill_index = jnp.where(upward >= 0, upward_rel, 2 * fine_count)
    gathered = spill_table[spill_index]
    lower = jnp.einsum(
        "nkcs,ksf->ncf",
        gathered[:, 0:2, :, 0:128],
        spill_parts[0:2, 0:128],
        preferred_element_type=jnp.float32,
    )
    upper = jnp.einsum(
        "nkcs,ksf->ncf",
        gathered[:, 2:7, :, 128:256],
        spill_parts[2:7, 128:256],
        preferred_element_type=jnp.float32,
    )
    hidden = finish_hidden(base, lower + upper, up_bias)
    group = 8
    valid = fine_neighbours >= 0
    in_own = (relative >= 0) & (relative < fine_count)
    in_prev = relative < 0
    weight_taps = jnp.transpose(conv_weight.reshape(cout, 27, cout), (1, 0, 2)).reshape(
        27 * cout, cout
    )
    sides = right_product(hidden, jnp.asarray(facet_matrix(), jnp.bfloat16)).astype(jnp.bfloat16)
    side_zero = jnp.zeros((1, cout, 384), jnp.bfloat16)
    arrived_sides = {}
    for offset in (1, -1):
        arrived_sides[offset] = passed_along(sides, ("row", "col"), offset)
    side_table = jnp.concatenate([sides, arrived_sides[1], arrived_sides[-1], side_zero], axis=0)
    side_index = jnp.where(
        in_own, relative, jnp.where(in_prev, relative + 2 * fine_count, relative + fine_count)
    )
    side_index = jnp.where(valid, side_index, 3 * fine_count)
    table_rows = side_table.shape[0]
    side_rows = jnp.transpose(side_table.reshape(table_rows, cout, 6, 64), (0, 2, 1, 3)).reshape(
        table_rows * 6, cout, 64
    )
    facet_pick = jnp.asarray(np.array(facet_choice(), np.int32))
    row_index = side_index * 6 + facet_pick[None, :]

    def conv_group(inputs):
        hidden_part, index_part = inputs
        chosen = side_rows[index_part]
        padded = place_sheets(hidden_part, chosen)
        return conv_finish(padded, weight_taps, conv_bias)

    result = lax.map(
        conv_group, (hidden.reshape(-1, group, cout, 512), row_index.reshape(-1, group, 26))
    )
    return result.reshape(fine_count, cout, 512)


def solution(mesh):
    in_specs = (
        P(("row", "col"), None, None),
        P(("row", "col"), None),
        P(("row", "col"), None),
        P(),
        P(),
        P(),
        P(),
    )
    out_specs = P(("row", "col"), None, None)
    return jax.shard_map(
        on_device, mesh=mesh, in_specs=in_specs, out_specs=out_specs, check_vma=False
    )
```

profile of v0, /device:TPU:6, one launch (start us, length us, event | category | flops | bytes accessed | tf_op | source)
XLA Modules:
  0.0 1652.4 jit_solution(5996794926322257763)
XLA Ops:
  10.5 11.2 fusion.48
  21.7 71.5 %fusion.12 = f32[96,32,4,4,3,3,9]{0,6,1,5,4,3,2:T(8,128)} fusion(f32[4,3,9,1,1,1,1,1]{2,0,1,7,6,5,4,3:T(4,128)S(1)} %copy-done.44, f32[96,4,4,4,3,3,3,32]{0,7,6,5,4,3,2,1:T(8,128)} %fusion.48), kind=kOutput, calls=%fused_computation.60 | convolution fusion | flops 573308928 | bytes 37159344 | tf_op jit(solution)/shard_map/bxyzuvwc,xui->bcyzvwi/dot_general | solution.py:121
  93.3 58.7 %fusion.15 = f32[96,32,9,9,4,3]{0,3,2,5,4,1:T(8,128)} fusion(f32[4,3,9,1,1,1,1]{2,0,1,6,5,4,3:T(4,128)S(1)} %copy-done.45, f32[96,32,4,4,3,3,9]{0,6,1,5,4,3,2:T(8,128)} %fusion.12), kind=kOutput, calls=%fused_computation.61 | convolution fusion | flops 429981696 | bytes 27869616 | tf_op jit(solution)/shard_map/bcyzvwi,yvj->bcijzw/dot_general | solution.py:122
  151.9 38.4 %bitcast_convert_fusion = bf16[96,32,9,9,9]{0,4,3,2,1:T(8,128)(2,1)S(1)} fusion(f32[4,3,9,1,1,1]{2,0,1,5,4,3:T(4,128)S(1)} %copy-done.46, f32[96,32,9,9,4,3]{0,3,2,5,4,1:T(8,128)} %fusion.15), kind=kOutput, calls=%fused_computation.55 | convolution fusion | flops 324725760 | bytes 16423344 | tf_op jit(solution)/shard_map/bcijzw,zwk->bcijk/dot_general | solution.py:123
  212.3 7.6 copy.329
  224.8 10.9 concatenate.162
  249.2 8.1 collective-permute-start.1
  262.2 13.1 collective-permute-done
  275.3 8.6 collective-permute-done.1
  288.2 8.0 collective-permute-start.2
  297.8 7.9 collective-permute-done.2
  307.1 13.2 gather_fusion.6
  322.4 4.9 multiply_convert_fusion
  329.6 8.1 collective-permute-start.4
  341.5 10.0 collective-permute-done.4
  351.5 8.1 collective-permute-done.3
  362.9 9.1 copy.339
  372.1 12.3 copy.340
  384.4 1266.5 %while.39 = (s32[]{:T(128)}, bf16[6,8,32,512]{3,2,1,0:T(8,128)(2,1)}, bf16[6,8,32,512]{3,2,1,0:T(8,128)(2,1)}, s32[6,8,26]{2,1,0:T(8,128)S(1)}, bf16[870,32,64]{...) while((s32[]{:T(128)}, ...), condition=%wide.region_7.8_spmd, body=%wide.region_6.7_spmd.sunk | while | flops 458720896 | bytes 213445840 | solution.py:264
  409.2 4.0 gather_fusion
  442.0 7.7 scatter.234
  449.7 7.6 scatter.235
  475.8 4.3 copy.493
  482.1 11.3 fusion.72
  493.4 7.2 fusion.73
  500.6 12.1 fusion.74
  585.1 27.9 %fusion.75 = bf16[8,32,800]{1,0,2:T(8,128)(2,1)S(1)} fusion(f32[8,1,32,800]{2,0,3,1:T(8,128)} %copy.495, f32[8,1,32,800]{2,0,3,1:T(8,128)} %copy.496, f32[8,1,32,800]{2,0,3,1:T(8,128)} %copy.497, f32[8,1,32,800]{2,0,3,1:T(8,128)} %copy.498, f32[8,1,32,800]{2,0,3,1:T(8,128)} %copy.499, f32[8,1,32,800]{2,0,3,1:T(8,128)} %copy.500, ...), kind=kLoop, calls=%fused_computation.15.clone.1 | loop fusion | flops 5734400 | bytes 22528128 | tf_op jit(solution)/shard_map/while/body/eval_jaxpr/convert_element_type | solution.py:178
  616.4 4.0 gather_fusion
  649.2 7.7 scatter.234
  656.9 7.6 scatter.235
  683.0 4.3 copy.493
  689.3 11.3 fusion.72
  700.6 7.2 fusion.73
  707.8 12.1 fusion.74
  792.3 27.9 %fusion.75 = bf16[8,32,800]{1,0,2:T(8,128)(2,1)S(1)} fusion(f32[8,1,32,800]{2,0,3,1:T(8,128)} %copy.495, f32[8,1,32,800]{2,0,3,1:T(8,128)} %copy.496, f32[8,1,32,800]{2,0,3,1:T(8,128)} %copy.497, f32[8,1,32,800]{2,0,3,1:T(8,128)} %copy.498, f32[8,1,32,800]{2,0,3,1:T(8,128)} %copy.499, f32[8,1,32,800]{2,0,3,1:T(8,128)} %copy.500, ...), kind=kLoop, calls=%fused_computation.15.clone.1 | loop fusion | flops 5734400 | bytes 22528128 | tf_op jit(solution)/shard_map/while/body/eval_jaxpr/convert_element_type | solution.py:178
  856.5 7.7 scatter.234
  864.1 7.6 scatter.235
  890.3 4.3 copy.493
  896.5 11.3 fusion.72
  907.8 7.2 fusion.73
  915.0 12.1 fusion.74
  999.5 27.9 %fusion.75 = bf16[8,32,800]{1,0,2:T(8,128)(2,1)S(1)} fusion(f32[8,1,32,800]{2,0,3,1:T(8,128)} %copy.495, f32[8,1,32,800]{2,0,3,1:T(8,128)} %copy.496, f32[8,1,32,800]{2,0,3,1:T(8,128)} %copy.497, f32[8,1,32,800]{2,0,3,1:T(8,128)} %copy.498, f32[8,1,32,800]{2,0,3,1:T(8,128)} %copy.499, f32[8,1,32,800]{2,0,3,1:T(8,128)} %copy.500, ...), kind=kLoop, calls=%fused_computation.15.clone.1 | loop fusion | flops 5734400 | bytes 22528128 | tf_op jit(solution)/shard_map/while/body/eval_jaxpr/convert_element_type | solution.py:178
  1030.8 4.0 gather_fusion
  1063.7 7.7 scatter.234
  1071.3 7.6 scatter.235
  1097.5 4.3 copy.493
  1103.7 11.3 fusion.72
  1115.1 7.2 fusion.73
  1122.2 12.1 fusion.74
  1206.7 27.9 %fusion.75 = bf16[8,32,800]{1,0,2:T(8,128)(2,1)S(1)} fusion(f32[8,1,32,800]{2,0,3,1:T(8,128)} %copy.495, f32[8,1,32,800]{2,0,3,1:T(8,128)} %copy.496, f32[8,1,32,800]{2,0,3,1:T(8,128)} %copy.497, f32[8,1,32,800]{2,0,3,1:T(8,128)} %copy.498, f32[8,1,32,800]{2,0,3,1:T(8,128)} %copy.499, f32[8,1,32,800]{2,0,3,1:T(8,128)} %copy.500, ...), kind=kLoop, calls=%fused_computation.15.clone.1 | loop fusion | flops 5734400 | bytes 22528128 | tf_op jit(solution)/shard_map/while/body/eval_jaxpr/convert_element_type | solution.py:178
  1270.9 7.7 scatter.234
  1278.6 7.6 scatter.235
  1304.7 4.3 copy.493
  1310.9 11.3 fusion.72
  1322.3 7.2 fusion.73
  1329.4 12.1 fusion.74
  1413.9 27.9 %fusion.75 = bf16[8,32,800]{1,0,2:T(8,128)(2,1)S(1)} fusion(f32[8,1,32,800]{2,0,3,1:T(8,128)} %copy.495, f32[8,1,32,800]{2,0,3,1:T(8,128)} %copy.496, f32[8,1,32,800]{2,0,3,1:T(8,128)} %copy.497, f32[8,1,32,800]{2,0,3,1:T(8,128)} %copy.498, f32[8,1,32,800]{2,0,3,1:T(8,128)} %copy.499, f32[8,1,32,800]{2,0,3,1:T(8,128)} %copy.500, ...), kind=kLoop, calls=%fused_computation.15.clone.1 | loop fusion | flops 5734400 | bytes 22528128 | tf_op jit(solution)/shard_map/while/body/eval_jaxpr/convert_element_type | solution.py:178
  1478.1 7.7 scatter.234
  1485.8 7.6 scatter.235
  1511.9 4.3 copy.493
  1518.1 11.3 fusion.72
  1529.5 7.2 fusion.73
  1536.7 12.1 fusion.74
  1621.2 27.9 %fusion.75 = bf16[8,32,800]{1,0,2:T(8,128)(2,1)S(1)} fusion(f32[8,1,32,800]{2,0,3,1:T(8,128)} %copy.495, f32[8,1,32,800]{2,0,3,1:T(8,128)} %copy.496, f32[8,1,32,800]{2,0,3,1:T(8,128)} %copy.497, f32[8,1,32,800]{2,0,3,1:T(8,128)} %copy.498, f32[8,1,32,800]{2,0,3,1:T(8,128)} %copy.499, f32[8,1,32,800]{2,0,3,1:T(8,128)} %copy.500, ...), kind=kLoop, calls=%fused_computation.15.clone.1 | loop fusion | flops 5734400 | bytes 22528128 | tf_op jit(solution)/shard_map/while/body/eval_jaxpr/convert_element_type | solution.py:178
  (1194 shorter events, 833.6 us)
Async XLA Ops:
  10.5 11.3 copy-start.44
  21.7 71.5 %copy-start.45 = (f32[4,3,9,1,1,1,1]{2,0,1,6,5,4,3:T(4,128)S(1)}, f32[4,3,9,1,1,1,1]{2,0,1,6,5,4,3:T(4,128)}, u32[]{:S(2)}) copy-start(f32[4,3,9,1,1,1,1]{2,0,1,6,5,4,3:T(4,128)} %constant.1116) | copy-start | bytes 1300
  93.3 58.7 %copy-start.46 = (f32[4,3,9,1,1,1]{2,0,1,5,4,3:T(4,128)S(1)}, f32[4,3,9,1,1,1]{2,0,1,5,4,3:T(4,128)}, u32[]{:S(2)}) copy-start(f32[4,3,9,1,1,1]{2,0,1,5,4,3:T(4,128)} %constant.1117) | copy-start | bytes 1300
  197.3 8.2 copy-start.38
  212.3 12.5 copy-start.34
  212.3 12.5 copy-start.35
  240.4 34.9 %collective-permute-start = (bf16[48,32,768]{2,1,0:T(8,128)(2,1)}, bf16[48,32,768]{2,1,0:T(8,128)(2,1)}, u32[]{:S(2)}, u32[]{:S(2)}) collective-permute-start(bf16[48,32,768]{2,1,0:T(8,128)(2,1)} %broadcast_select_fusion.1), channel_id=1, source_target_pairs={{0,1},{1,2},{2,3},{3,4},{4,5},{5,6},{6,7},{7,8},{8,9},{9,10},{10,1... | collective-permute-start | bytes 7077896 | tf_op jit(solution)/shard_map/ppermute | solution.py:22
  249.2 34.8 %collective-permute-start.1 = (bf16[48,32,768]{2,1,0:T(8,128)(2,1)}, bf16[48,32,768]{2,1,0:T(8,128)(2,1)}, u32[]{:S(2)}, u32[]{:S(2)}) collective-permute-start(bf16[48,32,768]{2,1,0:T(8,128)(2,1)} %broadcast_select_fusion), channel_id=1, source_target_pairs={{1,0},{2,1},{3,2},{4,3},{5,4},{6,5},{7,6},{8,7},{9,8},{10,9},{11,1... | collective-permute-start | bytes 7077896 | tf_op jit(solution)/shard_map/ppermute | solution.py:22
  262.1 34.1 %copy-start.48 = (s32[7]{0:T(128)S(1)}, s32[7]{0:T(128)}, u32[]{:S(2)}) copy-start(s32[7]{0:T(128)} %constant.1112) | copy-start | bytes 88
  262.2 34.1 %copy-start.36 = (s32[48,26]{0,1:T(8,128)S(1)}, s32[48,26]{0,1:T(8,128)}, u32[]{:S(2)}) copy-start(s32[48,26]{0,1:T(8,128)} %param.70) | copy-start | bytes 14980
  262.2 34.7 %copy-start.47 = (s32[26]{0:T(128)S(1)}, s32[26]{0:T(128)}, u32[]{:S(2)}) copy-start(s32[26]{0:T(128)} %constant.1096.clone) | copy-start | bytes 316
  288.2 17.5 %collective-permute-start.2 = (bf16[48,32,256]{2,1,0:T(8,128)(2,1)S(1)}, bf16[48,32,256]{2,1,0:T(8,128)(2,1)}, u32[]{:S(2)}, u32[]{:S(2)}) collective-permute-start(bf16[48,32,256]{2,1,0:T(8,128)(2,1)S(1)} %slice.1826), channel_id=1, source_target_pairs={{1,0},{2,1},{3,2},{4,3},{5,4},{6,5},{7,6},{8,7},{9,8},{10,9},{11,1... | collective-permute-start | bytes 2359304 | tf_op jit(solution)/shard_map/ppermute | solution.py:22
  307.1 13.3 copy-start.39
  327.2 12.6 copy-start.42
  329.6 21.8 %collective-permute-start.4 = (bf16[48,32,384]{2,1,0:T(8,128)(2,1)S(1)}, bf16[48,32,384]{2,1,0:T(8,128)(2,1)S(1)}, u32[]{:S(2)}, u32[]{:S(2)}) collective-permute-start(bf16[48,32,384]{2,1,0:T(8,128)(2,1)S(1)} %convolution_convert_fusion), channel_id=1, source_target_pairs={{1,0},{2,1},{3,2},{4,3},{5,4},{6,5},{7,6},{8,7},{9,8},{10,9},{11,1... | collective-permute-start | bytes 3538952 | tf_op jit(solution)/shard_map/ppermute | solution.py:22
  337.8 21.8 %collective-permute-start.3 = (bf16[48,32,384]{2,1,0:T(8,128)(2,1)S(1)}, bf16[48,32,384]{2,1,0:T(8,128)(2,1)}, u32[]{:S(2)}, u32[]{:S(2)}) collective-permute-start(bf16[48,32,384]{2,1,0:T(8,128)(2,1)S(1)} %convolution_convert_fusion), channel_id=1, source_target_pairs={{0,1},{1,2},{2,3},{3,4},{4,5},{5,6},{6,7},{7,8},{8,9},{9,10},{10,1... | collective-permute-start | bytes 3538952 | tf_op jit(solution)/shard_map/ppermute | solution.py:22
  372.0 12.3 copy-start.43
  414.2 5.9 copy-start.26
  414.2 6.0 copy-start.25
  414.2 6.2 copy-start.24
  414.2 6.3 copy-start.23
  414.3 6.5 copy-start.22
  414.3 6.7 copy-start.21
  414.3 6.8 copy-start.20
  475.8 6.2 copy-start.37
  621.4 5.9 copy-start.26
  621.4 6.0 copy-start.25
  621.5 6.2 copy-start.24
  621.5 6.3 copy-start.23
  621.5 6.5 copy-start.22
  621.5 6.7 copy-start.21
  621.5 6.8 copy-start.20
  683.0 6.2 copy-start.37
  828.6 5.9 copy-start.26
  828.7 6.0 copy-start.25
  828.7 6.2 copy-start.24
  828.7 6.3 copy-start.23
  828.7 6.5 copy-start.22
  828.7 6.7 copy-start.21
  828.7 6.8 copy-start.20
  890.3 6.2 copy-start.37
  1035.9 5.9 copy-start.26
  1035.9 6.0 copy-start.25
  1035.9 6.2 copy-start.24
  1035.9 6.3 copy-start.23
  1035.9 6.5 copy-start.22
  1035.9 6.7 copy-start.21
  1035.9 6.8 copy-start.20
  1097.5 6.2 copy-start.37
  1243.1 5.9 copy-start.26
  1243.1 6.0 copy-start.25
  1243.1 6.2 copy-start.24
  1243.1 6.3 copy-start.23
  1243.1 6.5 copy-start.22
  1243.1 6.7 copy-start.21
  1243.1 6.8 copy-start.20
  1304.7 6.2 copy-start.37
  1450.3 6.0 copy-start.25
  1450.3 6.2 copy-start.24
  1450.3 6.3 copy-start.23
  1450.3 6.5 copy-start.22
  1450.3 6.7 copy-start.21
  1450.4 6.8 copy-start.20
  1511.9 6.2 copy-start.37
  (158 other events, 759.7 us)
where the time goes:
time: 1670 us; the launch traced here: 1650 us
  local copies, waits for them, and re-layouts  1110 us (66%)
  matrix products  259 us (16%)
  other arithmetic  180 us (11%)
  waiting for transfers between devices  47.8 us (3%)
  starting transfers between devices  28.1 us (2%)
  loops' own time  27.1 us (2%)
    while x558, local copies, waits for them, and re-layouts  434 us
    scatter x162, local copies, waits for them, and re-layouts, place_sheets(): padded = padded.at[(slice(None), slice(None)) + target].set(sheet)  339 us
    convert_element_type x6, other arithmetic, conv_finish(): total = (total + conv_bias[None, :, None]).astype(jnp.bfloat16)  167 us
    slice x6, local copies, waits for them, and re-layouts, conv_finish(): total = total + spread[:, code, :, shift_now:shift_now + 800]  72.8 us
    dot_general x1, matrix products, upsample(): jnp.einsum('bxyzuvwc,xui->bcyzvwi', shaped, placer, precision=highest)  71.5 us
    dot_general x6, matrix products, conv_finish(): jnp.einsum('oc,ncp->nop', weight_taps, padded, preferred_element_type=jnp...  68.1 us
    dot_general x1, matrix products, upsample(): second = jnp.einsum('bcyzvwi,yvj->bcijzw', first, placer, precision=highest)  58.7 us
    ppermute x5, waiting for transfers between devices, passed_along(): return lax.ppermute(block, axis, route)  47.8 us
  transfers between devices with their start and end apart: 5, of which 5 were waited for; matrix products, arithmetic and copies ran while one was open for 1% of the time, Pallas kernels for 0%

commit v1 on v0

v1 whole, which is shorter than its diff:
```python
import jax
import jax.numpy as jnp
from jax import lax
from jax.experimental import pallas as pl
from jax.experimental.pallas import tpu as pltpu
from jax.sharding import PartitionSpec as P

F32 = jnp.float32
BF16 = jnp.bfloat16
AXES = ("row", "col")
HALO = 12
OWN = 48
SLOTS = OWN + 3 * HALO
ACTIVE = OWN + 2 * HALO
REACH = 3 * OWN
EXTRA_AT = 9 * 256
CONV_K = EXTRA_AT + 5 * 128

direction_list = [
    (code // 9 - 1, code // 3 % 3 - 1, code % 3 - 1) for code in range(27) if code != 13
]
column_of = {delta: column for column, delta in enumerate(direction_list)}
upward_list = [(0, 0, 1), (0, 1, 0), (0, 1, 1), (1, 0, 0), (1, 0, 1), (1, 1, 0), (1, 1, 1)]
upward_columns = [column_of[delta] for delta in upward_list]

CLASSES = [
    ((0, 0), 256, 1024 - 256, {(0, 0): (1, 1)}),
    ((0, 1), 256, 1024, {(0, 0): (1, 2), (0, 1): (1, 0)}),
    ((1, 0), 0, 768, {(0, 0): (2, 1), (1, 0): (0, 1)}),
    ((1, 1), 0, 1280, {(0, 0): (2, 2), (0, 1): (2, 0), (1, 0): (0, 2), (1, 1): (0, 0)}),
]
SHIFT_AT = {(1, 0): 0, (0, 0): 512, (0, 1): 768, (1, 1): 1024}
HALO_AT = 256
class_starts = []
UP_K = 0
for _, low, high, _ in CLASSES:
    class_starts.append(UP_K)
    UP_K += high - low


def iota(shape, dim):
    return lax.broadcasted_iota(jnp.int32, shape, dim)


def pack_kernel(place_ref, feat_ref, local_ref, up1_ref, down1_ref, down2_ref, up2_ref, table, source):
    low_lane = iota((64, 128), 1) < 64
    low_row = iota((8, 128), 0) < 4
    table[96] = jnp.zeros((16, 256), BF16)

    def coarse_block(c, _):
        for pair in range(2):
            near = feat_ref[c, :, 128 * pair:128 * pair + 128].astype(F32)
            far = feat_ref[c, :, 256 + 128 * pair:384 + 128 * pair].astype(F32)
            top = jnp.where(low_lane, near, pltpu.roll(far, 64, 1))
            bottom = jnp.where(low_lane, pltpu.roll(near, 64, 1), far)
            turned = jnp.concatenate([top, bottom], axis=0).T
            for octant in range(8):
                ox, oy, oz = octant // 4, octant // 2 % 2, octant % 2
                sheets = []
                for y in range(4):
                    at = 64 * ox + 8 * (4 * oy + y)
                    sheets.append(turned[at:at + 8])
                halves = []
                for one, two in ((sheets[0], sheets[1]), (sheets[2], sheets[3])):
                    if oz == 0:
                        halves.append(jnp.where(low_row, one, pltpu.roll(two, 4, 0)))
                    else:
                        halves.append(jnp.where(low_row, pltpu.roll(one, 4, 0), two))
                table[c * 8 + octant, :, 128 * pair:128 * pair + 128] = jnp.concatenate(
                    halves, axis=0).astype(BF16)
        return 0

    lax.fori_loop(0, feat_ref.shape[0], coarse_block, 0)

    def clear(k, _):
        source[k] = 96
        return 0

    lax.fori_loop(0, REACH + 1, clear, 0, unroll=8)

    def invert(k, _):
        source[place_ref[k]] = k
        return 0

    lax.fori_loop(0, 96, invert, 0, unroll=8)

    for ref, start in ((local_ref, OWN - HALO), (up1_ref, 2 * OWN - HALO), (down1_ref, 0),
                       (down2_ref, 0), (up2_ref, 3 * OWN - HALO)):

        def slot(u, _, ref=ref, start=start):
            ref[u] = table[source[start + u]]
            return 0

        lax.fori_loop(0, ref.shape[0], slot, 0, unroll=4)


def weight_kernel(up_ref, conv_ref, up_out, conv_out):
    spread = (iota((32, 256), 0) == iota((32, 256), 1) % 32).astype(BF16)
    lane_x = iota((32, 256), 1) // 32
    zero = jnp.zeros((32, 256), F32)
    wide = jnp.dot(conv_ref[...], spread, preferred_element_type=F32)

    def tap_of(kx, ky, kz):
        at = 32 * (9 * kx + 3 * ky + kz)
        return wide[at:at + 32]

    for ky in range(3):
        for kz in range(3):
            taps = [tap_of(kx, ky, kz) for kx in range(3)]
            for x in range(8):
                value = zero
                for kx in range(3):
                    value = jnp.where(lane_x == x + 1 - kx, taps[kx], value)
                at = 256 * (3 * ky + kz) + 32 * x
                conv_out[at:at + 32] = value.astype(BF16)
    pairs = [((0, 0), (0, 1)), ((1, 0), (1, 1)), ((2, 0), (2, 1)), ((0, 2), (1, 2)), ((2, 2), None)]
    for tile, (even, odd) in enumerate(pairs):
        at = EXTRA_AT + 128 * tile

        def beyond(tap):
            return zero if tap is None else jnp.where(lane_x == 7, tap_of(2, *tap), zero)

        def before(tap):
            return zero if tap is None else jnp.where(lane_x == 0, tap_of(0, *tap), zero)

        conv_out[at:at + 32] = beyond(even).astype(BF16)
        conv_out[at + 32:at + 64] = before(odd).astype(BF16)
        conv_out[at + 64:at + 96] = beyond(odd).astype(BF16)
        conv_out[at + 96:at + 128] = before(even).astype(BF16)

    lane_f = iota((64, 256), 1) // 32
    zero_up = jnp.zeros((64, 256), F32)

    def up_tap(kx, ky, kz):
        code = 9 * kx + 3 * ky + kz
        return jnp.dot(up_ref[:, 32 * code:32 * code + 32], spread, preferred_element_type=F32)

    for (_, low, high, taps_of), start in zip(CLASSES, class_starts):
        for shift, at_lane in SHIFT_AT.items():
            if not low <= at_lane < high:
                continue
            at = start + at_lane - low
            taps = [up_tap(kx, *taps_of[shift]) for kx in range(3)]
            for x in range(4):
                value = zero_up
                for kx in range(3):
                    value = jnp.where(lane_f == 2 * x + kx - 1, taps[kx], value)
                up_out[at + 64 * x:at + 64 * x + 64] = value.astype(BF16)
        for number, shift in enumerate(((0, 0), (0, 1), (1, 0), (1, 1))):
            at = start + HALO_AT - low + 64 * number
            value = zero_up
            if shift in taps_of:
                value = jnp.where(lane_f == 7, up_tap(0, *taps_of[shift]), zero_up)
            up_out[at:at + 64] = value.astype(BF16)


def main_kernel(near7_ref, near26_ref, local_ref, up1_ref, down1_ref, down2_ref, up2_ref, up_w, up_b,
                conv_w, conv_b, out_ref, octs, shifted, hidden, patches):
    octs[SLOTS] = jnp.zeros((16, 256), F32)

    def join(parts):
        def body(u, _):
            total = local_ref[u].astype(F32)
            for ref, offset in parts:
                total = total + ref[u - offset].astype(F32)
            octs[u] = total
            return 0
        return body

    lax.fori_loop(0, HALO, join([(up1_ref, 0), (up2_ref, 0)]), 0, unroll=2)
    lax.fori_loop(HALO, OWN + HALO, join([(up1_ref, 0), (down1_ref, HALO)]), 0, unroll=4)
    lax.fori_loop(OWN + HALO, SLOTS, join([(down1_ref, HALO), (down2_ref, OWN + HALO)]), 0, unroll=2)

    def shift_z(value, beyond):
        last = iota(value.shape, 0) % 4 == 3
        return jnp.where(last, pltpu.roll(beyond, 3, 0), pltpu.roll(value, 15, 0))

    def shift_y(value, beyond):
        first = iota(value.shape, 0) < 4
        return pltpu.roll(jnp.where(first, beyond, value), 12, 0)

    low_lane16 = iota((16, 128), 1) < 64

    def spread_octant(h, _):
        at = [near7_ref[h * 7 + j] for j in range(7)]
        here, z_next, y_next, yz_next = octs[h], octs[at[0]], octs[at[1]], octs[at[2]]
        by_z = shift_z(here, z_next)
        shifted[h, :, 512:768] = here.astype(BF16)
        shifted[h, :, 768:1024] = by_z.astype(BF16)
        shifted[h, :, 0:256] = shift_y(here, y_next).astype(BF16)
        shifted[h, :, 1024:1280] = shift_y(by_z, shift_z(y_next, yz_next)).astype(BF16)
        x0, xz, xy, xyz = [octs[at[j], :, 0:128] for j in (3, 4, 5, 6)]
        x_by_z = shift_z(x0, xz)
        x_by_y = shift_y(x0, xy)
        x_by_yz = shift_y(x_by_z, shift_z(xy, xyz))
        shifted[h, :, 256:384] = jnp.where(low_lane16, x0, pltpu.roll(x_by_z, 64, 1)).astype(BF16)
        shifted[h, :, 384:512] = jnp.where(low_lane16, x_by_y, pltpu.roll(x_by_yz, 64, 1)).astype(BF16)
        return 0

    lax.fori_loop(0, ACTIVE, spread_octant, 0)

    hidden[:, ACTIVE] = jnp.zeros((2, 64, 128), F32)
    up_bias = up_b[...]

    def upsample(chunk, _):
        for ((py, pz), low, high, _), start in zip(CLASSES, class_starts):
            rows = shifted[pl.ds(chunk * 8, 8), :, low:high].reshape(128, high - low)
            value = jnp.dot(rows, up_w[start:start + high - low], preferred_element_type=F32) + up_bias
            half = 0.5 * value
            value = half + half * jnp.tanh(half)
            for b in range(8):
                for y in range(4):
                    part = value[16 * b + 4 * y:16 * b + 4 * y + 4]
                    for tile in range(2):
                        hidden[tile, chunk * 8 + b, pl.ds(8 * (2 * y + py) + pz, 4, stride=2), :] = (
                            part[:, 128 * tile:128 * tile + 128])
        return 0

    lax.fori_loop(0, ACTIVE // 8, upsample, 0)

    conv_bias = conv_b[...]
    row = iota((8, 128), 0)
    first_row, last_row = row == 0, row == 7
    low_lane8 = iota((8, 128), 1) < 64
    lane = iota((8, 128), 1)
    even_lane = (lane < 32) | (lane >= 96)
    low_lane32 = iota((32, 128), 1) < 64

    def shift_row(dz, value, beyond):
        if dz == 0:
            return value
        if dz == 1:
            return pltpu.roll(jnp.where(first_row, beyond, value), 7, 0)
        return pltpu.roll(jnp.where(last_row, beyond, value), 1, 0)

    def two(one, other):
        return jnp.concatenate([one, other], axis=0).astype(BF16)

    def build(base, b, k):
        at = {delta: near26_ref[b * 26 + column] for delta, column in column_of.items()}
        at[(0, 0, 0)] = b + HALO

        def sheet(delta, y, tile):
            return hidden[tile, at[delta], 8 * y:8 * y + 8, :]

        def side(dy, dz, y):
            return jnp.where(low_lane8, sheet((1, dy, dz), y, 0), sheet((-1, dy, dz), y, 1))

        def sheets(dz, take):
            listed = []
            for step in range(10):
                dy = -1 if step == 0 else (1 if step == 9 else 0)
                y = (step - 1) % 8
                beyond = None if dz == 0 else take(dy, dz, y)
                listed.append(shift_row(dz, take(dy, 0, y), beyond))
            return listed

        def put(values, ky, at_lane):
            for pair in range(4):
                patches[k, 16 * pair:16 * pair + 16, at_lane:at_lane + 128] = values[pair]

        def put_all(listed, lanes):
            even = [two(listed[2 * n], listed[2 * n + 1]) for n in range(5)]
            odd = [two(listed[2 * n + 1], listed[2 * n + 2]) for n in range(4)]
            put(even[0:4], 0, lanes[0])
            put(odd, 1, lanes[1])
            put(even[1:5], 2, lanes[2])

        for dz in (-1, 0, 1):
            for tile in range(2):
                listed = sheets(dz, lambda dy, dz_, y: sheet((0, dy, dz_), y, tile))
                put_all(listed, [256 * (3 * ky + dz + 1) + 128 * tile for ky in range(3)])
        sides = [sheets(dz, side) for dz in (-1, 0, 1)]
        joined = [jnp.where(even_lane, one, pltpu.roll(other, 64, 1)) for one, other in zip(sides[0], sides[1])]
        put_all(joined, [EXTRA_AT + 128 * ky for ky in range(3)])
        last = sides[2]
        paired = [jnp.where(even_lane, last[n], pltpu.roll(last[n + 1], 64, 1)) for n in range(8)]
        put([two(paired[2 * n], paired[2 * n + 1]) for n in range(4)], 0, EXTRA_AT + 384)
        put([two(last[2 * n + 2], last[2 * n + 3]) for n in range(4)], 0, EXTRA_AT + 512)

    def convolve(chunk, _):
        base = chunk * 4
        for k in range(4):
            build(base, base + k, k)
        value = jnp.dot(patches[...].reshape(256, CONV_K), conv_w[...], preferred_element_type=F32) + conv_bias
        for pair in range(2):
            for half in range(2):
                turned = value[128 * pair:128 * pair + 128, 128 * half:128 * half + 128].T
                for x in range(0, 4, 2):
                    one, other = turned[32 * x:32 * x + 32], turned[32 * x + 32:32 * x + 64]
                    at = 256 * half + 64 * x
                    b = base + 2 * pair
                    out_ref[b, :, at:at + 128] = jnp.where(
                        low_lane32, one, pltpu.roll(other, 64, 1)).astype(BF16)
                    out_ref[b + 1, :, at:at + 128] = jnp.where(
                        low_lane32, pltpu.roll(one, 64, 1), other).astype(BF16)
        return 0

    lax.fori_loop(0, OWN // 4, convolve, 0)


def passed_along(block, distance):
    devices = range(lax.axis_size(AXES))
    route = [(i - distance, i) for i in devices if i - distance in devices]
    return lax.ppermute(block, AXES, route)


VMEM = pl.BlockSpec(memory_space=pltpu.VMEM)
SMEM = pl.BlockSpec(memory_space=pltpu.SMEM)


def on_device(
    coarse_feat, coarse_children, fine_neighbours, up_weight, up_bias, conv_weight, conv_bias
):
    rank = lax.axis_index(AXES)
    children = coarse_children.reshape(-1)
    place = jnp.where(children >= 0, children - (rank - 1) * OWN, REACH)
    own_ids = rank * OWN + lax.broadcasted_iota(jnp.int32, (OWN, 1), 0)
    upward = fine_neighbours[:, jnp.array(upward_columns)]
    upward = jnp.where(upward >= 0, upward - own_ids, 0)
    before = passed_along(upward[OWN - HALO:], 1)
    after = passed_along(upward[:HALO], -1)
    upward = jnp.concatenate([before, upward, after], axis=0)
    near7 = jnp.where(upward > 0, upward + lax.broadcasted_iota(jnp.int32, (ACTIVE, 1), 0), SLOTS)
    near26 = jnp.where(fine_neighbours >= 0, fine_neighbours - (rank * OWN - HALO), ACTIVE)

    counts = (SLOTS, OWN + HALO, OWN + 2 * HALO, 2 * HALO, HALO)
    local, up1, down1, down2, up2 = pl.pallas_call(
        pack_kernel,
        out_shape=[jax.ShapeDtypeStruct((count, 16, 256), BF16) for count in counts],
        in_specs=[SMEM, VMEM],
        out_specs=[VMEM] * 5,
        scratch_shapes=[pltpu.VMEM((97, 16, 256), BF16), pltpu.SMEM((REACH + 8,), jnp.int32)],
        compiler_params=pltpu.CompilerParams(vmem_limit_bytes=24 * 2 ** 20),
        name="pack",
    )(place, coarse_feat)
    up1 = passed_along(up1, 1)
    down1 = passed_along(down1, -1)
    down2 = passed_along(down2, -2)
    up2 = passed_along(up2, 2)

    up_w, conv_w = pl.pallas_call(
        weight_kernel,
        out_shape=[jax.ShapeDtypeStruct((UP_K, 256), BF16), jax.ShapeDtypeStruct((CONV_K, 256), BF16)],
        in_specs=[VMEM, VMEM],
        out_specs=[VMEM, VMEM],
        compiler_params=pltpu.CompilerParams(vmem_limit_bytes=24 * 2 ** 20),
        cost_estimate=pl.CostEstimate(flops=10 ** 9, bytes_accessed=4 * 10 ** 6, transcendentals=0),
        name="weights",
    )(up_weight, conv_weight.T)

    return pl.pallas_call(
        main_kernel,
        out_shape=jax.ShapeDtypeStruct((OWN, 32, 512), BF16),
        in_specs=[SMEM, SMEM] + [VMEM] * 9,
        out_specs=VMEM,
        scratch_shapes=[
            pltpu.VMEM((SLOTS + 1, 16, 256), F32),
            pltpu.VMEM((ACTIVE, 16, 1280), BF16),
            pltpu.VMEM((2, ACTIVE + 1, 64, 128), F32),
            pltpu.VMEM((4, 64, CONV_K), BF16),
        ],
        compiler_params=pltpu.CompilerParams(vmem_limit_bytes=48 * 2 ** 20),
        name="convolutions",
    )(near7.reshape(-1), near26.reshape(-1), local, up1, down1, down2, up2,
      up_w, jnp.tile(up_bias, 8)[None, :], conv_w, jnp.tile(conv_bias, 8)[None, :])


def solution(mesh):
    in_specs = (
        P(AXES, None, None),
        P(AXES, None),
        P(AXES, None),
        P(),
        P(),
        P(),
        P(),
    )
    return jax.shard_map(
        on_device, mesh=mesh, in_specs=in_specs, out_specs=P(AXES, None, None), check_vma=False
    )
```

time: 1670 us -> 72.5 us (0.04); the launches traced: 1650 us -> 71.9 us
  local copies, waits for them, and re-layouts: 1110 us -> 8.33 us
  matrix products: 259 us -> 0 us
  other arithmetic: 180 us -> 2.85 us
  waiting for transfers between devices: 47.8 us -> 5.97 us
  Pallas kernels: 0 us -> 29 us
  loops' own time: 27.1 us -> 0 us
    while x558 -> x0, local copies, waits for them, and re-layouts: 434 us -> none
    scatter x168 -> x0, local copies, waits for them, and re-layouts: 344 us -> none  [the longest x162 339 us: place_sheets(): padded = padded.at[(slice(None), slice(None)) + target].set(sheet)]
    dot_general x14 -> x0, matrix products: 259 us -> none  [the longest x1 71.5 us: upsample(): jnp.einsum('bxyzuvwc,xui->bcyzvwi', shaped, placer, precision=highest)]
    convert_element_type x6 -> x0, other arithmetic: 167 us -> none  [conv_finish(): total = (total + conv_bias[None, :, None]).astype(jnp.bfloat16)]
    slice x198 -> x1, local copies, waits for them, and re-layouts: 164 us -> 0.67 us  [on_device(): before = passed_along(upward[OWN - HALO:], 1)]
    gather x12 -> x1, local copies, waits for them, and re-layouts: 47.1 us -> 1.27 us  [on_device(): upward = fine_neighbours[:, jnp.array(upward_columns)]]
    ppermute x5 -> x6, waiting for transfers between devices: 47.8 us -> 5.97 us  [passed_along(): return lax.ppermute(block, AXES, route)]
    reshape x21 -> x1, local copies, waits for them, and re-layouts: 39.1 us -> 0.12 us  [on_device(): near26.reshape(-1)]
  transfers between devices with their start and end apart: 5 -> 6, of which waited for: 5 -> 1; matrix products, arithmetic and copies ran while one was open for 1% -> 9% of each run, Pallas kernels for 0% -> 1%
where the time goes in v1:
time: 72.5 us; the launch traced here: 71.9 us
  Pallas kernels  29 us (40%)
  starting transfers between devices  25.7 us (35%)
  local copies, waits for them, and re-layouts  8.33 us (11%)
  waiting for transfers between devices  5.97 us (8%)
  other arithmetic  2.85 us (4%)
    ppermute x6, starting transfers between devices, passed_along(): return lax.ppermute(block, AXES, route)  25.7 us
    pallas_call x1, Pallas kernels, on_device(): pl.pallas_call(main_kernel, out_shape=jax.ShapeDtypeStruct((OWN, 32, 512)...  23.6 us
    ppermute x6, waiting for transfers between devices, passed_along(): return lax.ppermute(block, AXES, route)  5.97 us
    unnamed x11, local copies, waits for them, and re-layouts  4.96 us
    pallas_call x1, Pallas kernels, on_device(): pl.pallas_call(pack_kernel, out_shape=[jax.ShapeDtypeStruct((count, 16, 2...  4.56 us
  transfers between devices with their start and end apart: 6, of which 1 were waited for; matrix products, arithmetic and copies ran while one was open for 9% of the time, Pallas kernels for 1%

profile of v1, /device:TPU:6, one launch (start us, length us, event | category | flops | bytes accessed | tf_op | source)
XLA Modules:
  0.0 71.9 jit_solution(14256507009576901324)
XLA Ops:
  0.0 0.7 subtract_select_fusion.1
  0.7 0.1 copy.13
  0.8 0.1 select_n.31.place_ref
  0.9 0.0 copy-start
  0.9 1.1 %copy-done = bf16[12,64,512]{2,1,0:T(8,128)(2,1)S(1)} copy-done((bf16[12,64,512]{2,1,0:T(8,128)(2,1)S(1)}, bf16[12,64,512]{2,1,0:T(8,128)(2,1)}, u32[]{:S(2)}) %copy-start) | copy-done | bytes 786456
  2.0 4.6 %pack.1 = (bf16[84,16,256]{2,1,0:T(8,128)(2,1)S(1)}, bf16[60,16,256]{2,1,0:T(8,128)(2,1)}, bf16[72,16,256]{2,1,0:T(8,128)(2,1)}, bf16[24,16,256]{2,1,0:T(8,128)(2,1)}, bf16[12,16,256]{2,1,0:T(8,128)(2,1)S(1)}) custom-call(s32[96]{0:T(128)S(1)} %select_n.31.place_ref, bf16[12,64,512]{2,1,0:T(8,128)(2,1)S(1)} %copy-done), custom_call_target="tpu_custom_call" | custom-call | tf_op jit(solution)/shard_map/pack/pallas_call | solution.py:328
  6.6 0.0 copy-start.1
  6.6 0.8 %copy-done.1 = bf16[84,16,256]{2,1,0:T(8,128)(2,1)} copy-done((bf16[84,16,256]{2,1,0:T(8,128)(2,1)}, bf16[84,16,256]{2,1,0:T(8,128)(2,1)S(1)}, u32[]{:S(2)}) %copy-start.1) | copy-done | bytes 688152
  7.4 1.9 %collective-permute-start.2 = (bf16[60,16,256]{2,1,0:T(8,128)(2,1)}, bf16[60,16,256]{2,1,0:T(8,128)(2,1)}, u32[]{:S(2)}, u32[]{:S(2)}) collective-permute-start(bf16[60,16,256]{2,1,0:T(8,128)(2,1)} %get-tuple-element.13), channel_id=1, source_target_pairs={{0,1},{1,2},{2,3},{3,4},{4,5},{5,6},{6,7},{7,8},{8,9},{9,10},{10,1... | collective-permute-start | bytes 1474568 | tf_op jit(solution)/shard_map/ppermute | solution.py:305
  9.3 8.1 %collective-permute-start.3 = (bf16[72,16,256]{2,1,0:T(8,128)(2,1)}, bf16[72,16,256]{2,1,0:T(8,128)(2,1)}, u32[]{:S(2)}, u32[]{:S(2)}) collective-permute-start(bf16[72,16,256]{2,1,0:T(8,128)(2,1)} %get-tuple-element.14), channel_id=1, source_target_pairs={{1,0},{2,1},{3,2},{4,3},{5,4},{6,5},{7,6},{8,7},{9,8},{10,9},{11,1... | collective-permute-start | bytes 1769480 | tf_op jit(solution)/shard_map/ppermute | solution.py:305
  17.5 0.7 pad_clamp_fusion
  18.1 1.3 %gather_fusion = s32[7,48]{1,0:T(8,128)S(1)} fusion(s32[48,26]{0,1:T(8,128)} %param.10, s32[1024]{0:T(1024)S(1)} %pad_clamp_fusion), kind=kCustom, calls=%fused_computation | custom fusion | bytes 2716 | tf_op jit(solution)/shard_map/gather | solution.py:319
  19.4 0.7 fusion
  20.1 1.9 %collective-permute-start = (s32[12,7]{0,1:T(8,128)}, s32[12,7]{0,1:T(8,128)S(1)}, u32[]{:S(2)}, u32[]{:S(2)}) collective-permute-start(s32[12,7]{0,1:T(8,128)} %get-tuple-element.19), channel_id=1, source_target_pairs={{0,1},{1,2},{2,3},{3,4},{4,5},{5,6},{6,7},{7,8},{8,9},{9,10},{10,1... | collective-permute-start | bytes 1016 | tf_op jit(solution)/shard_map/ppermute | solution.py:305
  22.0 7.9 %collective-permute-start.1 = (s32[12,7]{0,1:T(8,128)}, s32[12,7]{0,1:T(8,128)}, u32[]{:S(2)}, u32[]{:S(2)}) collective-permute-start(s32[12,7]{0,1:T(8,128)} %get-tuple-element.20), channel_id=1, source_target_pairs={{1,0},{2,1},{3,2},{4,3},{5,4},{6,5},{7,6},{8,7},{9,8},{10,9},{11,1... | collective-permute-start | bytes 1016 | tf_op jit(solution)/shard_map/ppermute | solution.py:305
  29.9 1.9 %collective-permute-start.4 = (bf16[24,16,256]{2,1,0:T(8,128)(2,1)}, bf16[24,16,256]{2,1,0:T(8,128)(2,1)}, u32[]{:S(2)}, u32[]{:S(2)}) collective-permute-start(bf16[24,16,256]{2,1,0:T(8,128)(2,1)} %get-tuple-element.15), channel_id=1, source_target_pairs={{2,0},{3,1},{4,2},{5,3},{6,4},{7,5},{8,6},{9,7},{10,8},{11,9},{12,... | collective-permute-start | bytes 589832 | tf_op jit(solution)/shard_map/ppermute | solution.py:305
  31.8 1.0 %copy.14 = bf16[32,864]{0,1:T(8,128)(2,1)S(1)} copy(bf16[32,864]{1,0:T(8,128)(2,1)} %param.13) | data formatting | bytes 110592 | tf_op args[5]
  32.8 0.7 %subtract_select_fusion = s32[48,26]{0,1:T(8,128)S(1)} fusion(s32[48,26]{0,1:T(8,128)} %param.10, s32[]{:T(128)S(6)} %sub.29), kind=kLoop, calls=%fused_computation.1 | loop fusion | flops 3744 | bytes 9988 | tf_op jit(solution)/shard_map/jit(_where)/select_n | solution.py:325
  33.5 0.0 copy-start.3
  33.5 0.9 %copy-done.3 = bf16[64,864]{1,0:T(8,128)(2,1)S(1)} copy-done((bf16[64,864]{1,0:T(8,128)(2,1)S(1)}, bf16[64,864]{1,0:T(8,128)(2,1)}, u32[]{:S(2)}) %copy-start.3) | copy-done | bytes 110616
  34.4 0.0 copy-start.4
  34.4 0.9 %weights.1 = (bf16[3328,256]{1,0:T(8,128)(2,1)S(1)}, bf16[2944,256]{1,0:T(8,128)(2,1)S(1)}) custom-call(bf16[64,864]{1,0:T(8,128)(2,1)S(1)} %copy-done.3, bf16[864,32]{1,0:T(8,128)(2,1)S(1)} %bitcast.3), custom_call_target="tpu_custom_call" | custom-call | flops 1000000000 | bytes 4000000 | tf_op jit(solution)/shard_map/weights/pallas_call | solution.py:342
  35.3 0.0 copy-done.4
  35.3 0.1 broadcast_in_dim_tile.6.up_b
  35.4 0.7 tile.5
  36.1 0.1 broadcast_in_dim_tile.7.conv_b
  36.2 0.1 copy.12
  36.2 0.1 reshape.25.near26_ref
  36.4 0.0 collective-permute-done
  36.4 3.9 %collective-permute-start.5 = (bf16[12,16,256]{2,1,0:T(8,128)(2,1)S(1)}, bf16[12,16,256]{2,1,0:T(8,128)(2,1)S(1)}, u32[]{:S(2)}, u32[]{:S(2)}) collective-permute-start(bf16[12,16,256]{2,1,0:T(8,128)(2,1)S(1)} %get-tuple-element.16), channel_id=1, source_target_pairs={{0,2},{1,3},{2,4},{3,5},{4,6},{5,7},{6,8},{7,9},{8,10},{9,11},{10,... | collective-permute-start | bytes 294920 | tf_op jit(solution)/shard_map/ppermute | solution.py:305
  40.3 0.0 collective-permute-done.1
  40.3 0.8 %add_select_fusion = s32[72,7]{0,1:T(8,128)S(1)} fusion(s32[12,7]{0,1:T(8,128)} %collective-permute-done.1, s32[48,7]{0,1:T(8,128)S(1)} %select_bitcast_fusion, s32[12,7]{0,1:T(8,128)S(1)} %collective-permute-done), kind=kLoop, calls=%fused_computation.6 | loop fusion | flops 2520 | bytes 4032 | tf_op jit(solution)/shard_map/jit(_where)/select_n | solution.py:324
  41.1 0.1 copy.11
  41.2 0.1 select_n.28.near7_ref
  41.3 6.0 %collective-permute-done.5.up2_ref = bf16[12,16,256]{2,1,0:T(8,128)(2,1)S(1)} collective-permute-done((bf16[12,16,256]{2,1,0:T(8,128)(2,1)S(1)}, bf16[12,16,256]{2,1,0:T(8,128)(2,1)S(1)}, u32[]{:S(2)}, u32[]{:S(2)}) %collective-permute-start.5) | collective-permute-done | bytes 98336 | tf_op jit(solution)/shard_map/ppermute | solution.py:305
  47.3 0.0 collective-permute-done.4.down2_ref
  47.3 0.0 collective-permute-done.2.up1_ref
  47.3 0.0 collective-permute-done.3.down1_ref
  47.3 0.0 copy-start.2
  47.3 1.1 %copy-done.2 = bf16[84,16,256]{2,1,0:T(8,128)(2,1)S(1)} copy-done((bf16[84,16,256]{2,1,0:T(8,128)(2,1)S(1)}, bf16[84,16,256]{2,1,0:T(8,128)(2,1)}, u32[]{:S(2)}) %copy-start.2) | copy-done | bytes 688152
  48.4 23.6 %convolutions.1 = bf16[48,32,512]{2,1,0:T(8,128)(2,1)} custom-call(s32[504]{0:T(512)S(1)} %select_n.28.near7_ref, s32[1248]{0:T(1024)S(1)} %reshape.25.near26_ref, bf16[84,16,256]{2,1,0:T(8,128)(2,1)S(1)} %copy-done.2, bf16[60,16,256]{2,1,0:T(8,128)(2,1)} %collective-permute-done.2.up1_ref, bf16[72,16,256]{2,1,0:T(8,128)(2,1)} %collective-permute-done.3.down1_ref, ...), custom_call_target="tpu_custom_call" | custom-call | tf_op jit(solution)/shard_map/convolutions/pallas_call | solution.py:352
  (3 shorter events, 0.0 us)
Async XLA Ops:
  0.9 1.1 %copy-start = (bf16[12,64,512]{2,1,0:T(8,128)(2,1)S(1)}, bf16[12,64,512]{2,1,0:T(8,128)(2,1)}, u32[]{:S(2)}) copy-start(bf16[12,64,512]{2,1,0:T(8,128)(2,1)} %feat_ref.1) | copy-start | bytes 2359300
  6.6 0.8 %copy-start.1 = (bf16[84,16,256]{2,1,0:T(8,128)(2,1)}, bf16[84,16,256]{2,1,0:T(8,128)(2,1)S(1)}, u32[]{:S(2)}) copy-start(bf16[84,16,256]{2,1,0:T(8,128)(2,1)S(1)} %get-tuple-element.12.local_ref) | copy-start | bytes 2064388
  7.4 39.9 %collective-permute-start.2 = (bf16[60,16,256]{2,1,0:T(8,128)(2,1)}, bf16[60,16,256]{2,1,0:T(8,128)(2,1)}, u32[]{:S(2)}, u32[]{:S(2)}) collective-permute-start(bf16[60,16,256]{2,1,0:T(8,128)(2,1)} %get-tuple-element.13), channel_id=1, source_target_pairs={{0,1},{1,2},{2,3},{3,4},{4,5},{5,6},{6,7},{7,8},{8,9},{9,10},{10,1... | collective-permute-start | bytes 1474568 | tf_op jit(solution)/shard_map/ppermute | solution.py:305
  9.3 38.0 %collective-permute-start.3 = (bf16[72,16,256]{2,1,0:T(8,128)(2,1)}, bf16[72,16,256]{2,1,0:T(8,128)(2,1)}, u32[]{:S(2)}, u32[]{:S(2)}) collective-permute-start(bf16[72,16,256]{2,1,0:T(8,128)(2,1)} %get-tuple-element.14), channel_id=1, source_target_pairs={{1,0},{2,1},{3,2},{4,3},{5,4},{6,5},{7,6},{8,7},{9,8},{10,9},{11,1... | collective-permute-start | bytes 1769480 | tf_op jit(solution)/shard_map/ppermute | solution.py:305
  20.1 16.3 %collective-permute-start = (s32[12,7]{0,1:T(8,128)}, s32[12,7]{0,1:T(8,128)S(1)}, u32[]{:S(2)}, u32[]{:S(2)}) collective-permute-start(s32[12,7]{0,1:T(8,128)} %get-tuple-element.19), channel_id=1, source_target_pairs={{0,1},{1,2},{2,3},{3,4},{4,5},{5,6},{6,7},{7,8},{8,9},{9,10},{10,1... | collective-permute-start | bytes 1016 | tf_op jit(solution)/shard_map/ppermute | solution.py:305
  22.0 18.3 %collective-permute-start.1 = (s32[12,7]{0,1:T(8,128)}, s32[12,7]{0,1:T(8,128)}, u32[]{:S(2)}, u32[]{:S(2)}) collective-permute-start(s32[12,7]{0,1:T(8,128)} %get-tuple-element.20), channel_id=1, source_target_pairs={{1,0},{2,1},{3,2},{4,3},{5,4},{6,5},{7,6},{8,7},{9,8},{10,9},{11,1... | collective-permute-start | bytes 1016 | tf_op jit(solution)/shard_map/ppermute | solution.py:305
  29.9 17.4 %collective-permute-start.4 = (bf16[24,16,256]{2,1,0:T(8,128)(2,1)}, bf16[24,16,256]{2,1,0:T(8,128)(2,1)}, u32[]{:S(2)}, u32[]{:S(2)}) collective-permute-start(bf16[24,16,256]{2,1,0:T(8,128)(2,1)} %get-tuple-element.15), channel_id=1, source_target_pairs={{2,0},{3,1},{4,2},{5,3},{6,4},{7,5},{8,6},{9,7},{10,8},{11,9},{12,... | collective-permute-start | bytes 589832 | tf_op jit(solution)/shard_map/ppermute | solution.py:305
  33.5 0.9 %copy-start.3 = (bf16[64,864]{1,0:T(8,128)(2,1)S(1)}, bf16[64,864]{1,0:T(8,128)(2,1)}, u32[]{:S(2)}) copy-start(bf16[64,864]{1,0:T(8,128)(2,1)} %up_ref.1) | copy-start | bytes 331780
  34.4 0.9 %copy-start.4 = (f32[32]{0:T(128)S(1)}, f32[32]{0:T(128)}, u32[]{:S(2)}) copy-start(f32[32]{0:T(128)} %param.12) | copy-start | bytes 388
  36.4 10.9 %collective-permute-start.5 = (bf16[12,16,256]{2,1,0:T(8,128)(2,1)S(1)}, bf16[12,16,256]{2,1,0:T(8,128)(2,1)S(1)}, u32[]{:S(2)}, u32[]{:S(2)}) collective-permute-start(bf16[12,16,256]{2,1,0:T(8,128)(2,1)S(1)} %get-tuple-element.16), channel_id=1, source_target_pairs={{0,2},{1,3},{2,4},{3,5},{4,6},{5,7},{6,8},{7,9},{8,10},{9,11},{10,... | collective-permute-start | bytes 294920 | tf_op jit(solution)/shard_map/ppermute | solution.py:305
  47.3 1.1 %copy-start.2 = (bf16[84,16,256]{2,1,0:T(8,128)(2,1)S(1)}, bf16[84,16,256]{2,1,0:T(8,128)(2,1)}, u32[]{:S(2)}) copy-start(bf16[84,16,256]{2,1,0:T(8,128)(2,1)} %copy-done.1) | copy-start | bytes 2064388

commit v2 on v1

--- a/solution.py
+++ b/solution.py
@@ -13,6 +13,9 @@
 SLOTS = OWN + 3 * HALO
 ACTIVE = OWN + 2 * HALO
 REACH = 3 * OWN
+SPREAD = 4
+UP = 24
+GROUP = 4
 EXTRA_AT = 9 * 256
 CONV_K = EXTRA_AT + 5 * 128
 
@@ -42,7 +45,32 @@
     return lax.broadcasted_iota(jnp.int32, shape, dim)
 
 
-def pack_kernel(place_ref, feat_ref, local_ref, up1_ref, down1_ref, down2_ref, up2_ref, table, source):
+def exchange_kernel(children_ref, near_ref, feat_ref, up_ref, conv_ref, octs_ref, near_out, up_hbm, conv_hbm,
+                    table, slots, source_v, source, from1, from_1, from_2, from2, near_prev, near_next,
+                    up_out, conv_out, send_sem, recv_sem, local_sem, weight_sem):
+    ranks = lax.axis_size("row") * lax.axis_size("col")
+    rank = lax.axis_index("row") * lax.axis_size("col") + lax.axis_index("col")
+
+    def device(offset):
+        other = lax.rem(rank + offset + ranks, ranks)
+        return other // lax.axis_size("col"), lax.rem(other, lax.axis_size("col"))
+
+    barrier = pltpu.get_barrier_semaphore()
+    for offset in (1, -1, 2, -2):
+        pl.semaphore_signal(barrier, inc=1, device_id=device(offset), device_id_type=pl.DeviceIdType.MESH)
+
+    slot_id = iota((8, 128), 0) * 128 + iota((8, 128), 1)
+    first = (rank - 1) * OWN
+    chosen = jnp.full((8, 128), 96, jnp.int32)
+    for c in range(12):
+        for o in range(8):
+            child = children_ref[c, o]
+            position = jnp.where(child >= 0, child - first, REACH)
+            chosen = jnp.where(slot_id == position, 8 * c + o, chosen)
+    source_v[...] = chosen
+    fetch = pltpu.make_async_copy(source_v, source, local_sem)
+    fetch.start()
+
     low_lane = iota((64, 128), 1) < 64
     low_row = iota((8, 128), 0) < 4
     table[96] = jnp.zeros((16, 256), BF16)
@@ -72,33 +100,69 @@
 
     lax.fori_loop(0, feat_ref.shape[0], coarse_block, 0)
 
-    def clear(k, _):
-        source[k] = 96
+    fetch.wait()
+
+    def fill(k, _):
+        for j in range(4):
+            q = k * 4 + j
+            slots[q] = table[source[q // 128, q % 128]]
         return 0
 
-    lax.fori_loop(0, REACH + 1, clear, 0, unroll=8)
-
-    def invert(k, _):
-        source[place_ref[k]] = k
-        return 0
-
-    lax.fori_loop(0, 96, invert, 0, unroll=8)
-
-    for ref, start in ((local_ref, OWN - HALO), (up1_ref, 2 * OWN - HALO), (down1_ref, 0),
-                       (down2_ref, 0), (up2_ref, 3 * OWN - HALO)):
-
-        def slot(u, _, ref=ref, start=start):
-            ref[u] = table[source[start + u]]
+    lax.fori_loop(0, REACH // 4, fill, 0)
+
+    pl.semaphore_wait(barrier, 4)
+    copies = []
+    for number, (src, dst, offset) in enumerate((
+            (slots.at[0:OWN + 2 * HALO], from_1, -1),
+            (slots.at[2 * OWN - HALO:REACH], from1, 1),
+            (slots.at[0:2 * HALO], from_2, -2),
+            (slots.at[REACH - HALO:REACH], from2, 2),
+            (near_ref.at[0:16], near_next, -1),
+            (near_ref.at[OWN - 16:OWN], near_prev, 1))):
+        copy = pltpu.make_async_remote_copy(
+            src_ref=src, dst_ref=dst, send_sem=send_sem.at[number], recv_sem=recv_sem.at[number],
+            device_id=device(offset), device_id_type=pl.DeviceIdType.MESH)
+        copy.start()
+        copies.append(copy)
+
+    make_weights(up_ref, conv_ref, up_out, conv_out)
+    up_copy = pltpu.make_async_copy(up_out, up_hbm, weight_sem.at[0])
+    conv_copy = pltpu.make_async_copy(conv_out, conv_hbm, weight_sem.at[1])
+    up_copy.start()
+    conv_copy.start()
+
+    def relative(value):
+        moved = value - (rank * OWN - HALO)
+        return jnp.where((value >= 0) & (moved >= 0) & (moved < SLOTS), moved, SLOTS)
+
+    near_out[16:16 + OWN] = relative(near_ref[...])
+    octs_ref[SLOTS] = jnp.zeros((16, 256), F32)
+    for copy in copies[4:] + copies[:4]:
+        copy.wait()
+    near_out[0:16] = relative(near_prev[...])
+    near_out[16 + OWN:32 + OWN] = relative(near_next[...])
+
+    def join(parts):
+        def body(u, _):
+            total = slots[u + OWN - HALO].astype(F32)
+            for ref, offset in parts:
+                total = total + ref[u - offset].astype(F32)
+            octs_ref[u] = total
             return 0
-
-        lax.fori_loop(0, ref.shape[0], slot, 0, unroll=4)
-
-
-def weight_kernel(up_ref, conv_ref, up_out, conv_out):
+        return body
+
+    lax.fori_loop(0, HALO, join([(from1, 0), (from2, 0)]), 0, unroll=4)
+    lax.fori_loop(HALO, OWN + HALO, join([(from1, 0), (from_1, HALO)]), 0, unroll=8)
+    lax.fori_loop(OWN + HALO, SLOTS, join([(from_1, HALO), (from_2, OWN + HALO)]), 0, unroll=4)
+    up_copy.wait()
+    conv_copy.wait()
+
+
+def make_weights(up_ref, conv_ref, up_out, conv_out):
     spread = (iota((32, 256), 0) == iota((32, 256), 1) % 32).astype(BF16)
     lane_x = iota((32, 256), 1) // 32
     zero = jnp.zeros((32, 256), F32)
-    wide = jnp.dot(conv_ref[...], spread, preferred_element_type=F32)
+    wide = lax.dot_general(conv_ref[...], spread, (((0,), (0,)), ((), ())), preferred_element_type=F32)
 
     def tap_of(kx, ky, kz):
         at = 32 * (9 * kx + 3 * ky + kz)
@@ -154,22 +218,17 @@
             up_out[at:at + 64] = value.astype(BF16)
 
 
-def main_kernel(near7_ref, near26_ref, local_ref, up1_ref, down1_ref, down2_ref, up2_ref, up_w, up_b,
-                conv_w, conv_b, out_ref, octs, shifted, hidden, patches):
-    octs[SLOTS] = jnp.zeros((16, 256), F32)
-
-    def join(parts):
-        def body(u, _):
-            total = local_ref[u].astype(F32)
-            for ref, offset in parts:
-                total = total + ref[u - offset].astype(F32)
-            octs[u] = total
-            return 0
-        return body
-
-    lax.fori_loop(0, HALO, join([(up1_ref, 0), (up2_ref, 0)]), 0, unroll=2)
-    lax.fori_loop(HALO, OWN + HALO, join([(up1_ref, 0), (down1_ref, HALO)]), 0, unroll=4)
-    lax.fori_loop(OWN + HALO, SLOTS, join([(down1_ref, HALO), (down2_ref, OWN + HALO)]), 0, unroll=2)
+def main_kernel(near_ref, octs, up_hbm, up_b, conv_hbm, conv_b, out_ref, up_w, conv_w, shifted, hidden,
+                patches_0, patches_1, weight_sem):
+    up_copy = pltpu.make_async_copy(up_hbm, up_w, weight_sem.at[0])
+    conv_copy = pltpu.make_async_copy(conv_hbm, conv_w, weight_sem.at[1])
+    up_copy.start()
+    conv_copy.start()
+    spread = (iota((32, 256), 0) == iota((32, 256), 1) % 32).astype(F32)
+
+    def wide_bias(ref):
+        return jnp.dot(jnp.broadcast_to(ref[...], (8, 32)), spread, precision=lax.Precision.HIGHEST,
+                       preferred_element_type=F32)[0:1]
 
     def shift_z(value, beyond):
         last = iota(value.shape, 0) % 4 == 3
@@ -181,44 +240,53 @@
 
     low_lane16 = iota((16, 128), 1) < 64
 
-    def spread_octant(h, _):
-        at = [near7_ref[h * 7 + j] for j in range(7)]
+    def spread_octant(h):
+        at = [near_ref[h + 4, column] for column in upward_columns]
         here, z_next, y_next, yz_next = octs[h], octs[at[0]], octs[at[1]], octs[at[2]]
         by_z = shift_z(here, z_next)
-        shifted[h, :, 512:768] = here.astype(BF16)
-        shifted[h, :, 768:1024] = by_z.astype(BF16)
-        shifted[h, :, 0:256] = shift_y(here, y_next).astype(BF16)
-        shifted[h, :, 1024:1280] = shift_y(by_z, shift_z(y_next, yz_next)).astype(BF16)
         x0, xz, xy, xyz = [octs[at[j], :, 0:128] for j in (3, 4, 5, 6)]
         x_by_z = shift_z(x0, xz)
         x_by_y = shift_y(x0, xy)
         x_by_yz = shift_y(x_by_z, shift_z(xy, xyz))
-        shifted[h, :, 256:384] = jnp.where(low_lane16, x0, pltpu.roll(x_by_z, 64, 1)).astype(BF16)
-        shifted[h, :, 384:512] = jnp.where(low_lane16, x_by_y, pltpu.roll(x_by_yz, 64, 1)).astype(BF16)
+        return [
+            (0, shift_y(here, y_next)),
+            (256, jnp.where(low_lane16, x0, pltpu.roll(x_by_z, 64, 1))),
+            (384, jnp.where(low_lane16, x_by_y, pltpu.roll(x_by_yz, 64, 1))),
+            (512, here),
+            (768, by_z),
+            (1024, shift_y(by_z, shift_z(y_next, yz_next))),
+        ]
+
+    def spread_octants(group, _):
+        for h, parts in [(group * SPREAD + k, spread_octant(group * SPREAD + k)) for k in range(SPREAD)]:
+            for lane, value in parts:
+                shifted[h, :, lane:lane + value.shape[1]] = value.astype(BF16)
         return 0
 
-    lax.fori_loop(0, ACTIVE, spread_octant, 0)
-
-    hidden[:, ACTIVE] = jnp.zeros((2, 64, 128), F32)
-    up_bias = up_b[...]
+    lax.fori_loop(0, ACTIVE // SPREAD, spread_octants, 0)
+    up_copy.wait()
+
+    hidden[:, SLOTS] = jnp.zeros((2, 64, 128), F32)
+    up_bias = wide_bias(up_b)
 
     def upsample(chunk, _):
         for ((py, pz), low, high, _), start in zip(CLASSES, class_starts):
-            rows = shifted[pl.ds(chunk * 8, 8), :, low:high].reshape(128, high - low)
+            rows = shifted[pl.ds(chunk * UP, UP), :, low:high].reshape(16 * UP, high - low)
             value = jnp.dot(rows, up_w[start:start + high - low], preferred_element_type=F32) + up_bias
             half = 0.5 * value
             value = half + half * jnp.tanh(half)
-            for b in range(8):
+            for b in range(UP):
                 for y in range(4):
                     part = value[16 * b + 4 * y:16 * b + 4 * y + 4]
                     for tile in range(2):
-                        hidden[tile, chunk * 8 + b, pl.ds(8 * (2 * y + py) + pz, 4, stride=2), :] = (
+                        hidden[tile, chunk * UP + b, pl.ds(8 * (2 * y + py) + pz, 4, stride=2), :] = (
                             part[:, 128 * tile:128 * tile + 128])
         return 0
 
-    lax.fori_loop(0, ACTIVE // 8, upsample, 0)
-
-    conv_bias = conv_b[...]
+    lax.fori_loop(0, ACTIVE // UP, upsample, 0)
+    conv_copy.wait()
+
+    conv_bias = wide_bias(conv_b)
     row = iota((8, 128), 0)
     first_row, last_row = row == 0, row == 7
     low_lane8 = iota((8, 128), 1) < 64
@@ -236,8 +304,8 @@
     def two(one, other):
         return jnp.concatenate([one, other], axis=0).astype(BF16)
 
-    def build(base, b, k):
-        at = {delta: near26_ref[b * 26 + column] for delta, column in column_of.items()}
+    def build(patches, b, k):
+        at = {delta: near_ref[b + 16, column] for delta, column in column_of.items()}
         at[(0, 0, 0)] = b + HALO
 
         def sheet(delta, y, tile):
@@ -278,12 +346,9 @@
         put([two(paired[2 * n], paired[2 * n + 1]) for n in range(4)], 0, EXTRA_AT + 384)
         put([two(last[2 * n + 2], last[2 * n + 3]) for n in range(4)], 0, EXTRA_AT + 512)
 
-    def convolve(chunk, _):
-        base = chunk * 4
-        for k in range(4):
-            build(base, base + k, k)
-        value = jnp.dot(patches[...].reshape(256, CONV_K), conv_w[...], preferred_element_type=F32) + conv_bias
-        for pair in range(2):
+    def convolve(patches, base):
+        value = jnp.dot(patches[...].reshape(64 * GROUP, CONV_K), conv_w[...], preferred_element_type=F32) + conv_bias
+        for pair in range(GROUP // 2):
             for half in range(2):
                 turned = value[128 * pair:128 * pair + 128, 128 * half:128 * half + 128].T
                 for x in range(0, 4, 2):
@@ -294,76 +359,81 @@
                         low_lane32, one, pltpu.roll(other, 64, 1)).astype(BF16)
                     out_ref[b + 1, :, at:at + 128] = jnp.where(
                         low_lane32, pltpu.roll(one, 64, 1), other).astype(BF16)
+
+    def build_group(patches, base):
+        for k in range(GROUP):
+            build(patches, base + k, k)
+
+    build_group(patches_0, 0)
+
+    def groups(step, _):
+        base = step * 2 * GROUP
+        build_group(patches_1, base + GROUP)
+        convolve(patches_0, base)
+        build_group(patches_0, jnp.minimum(base + 2 * GROUP, OWN - GROUP))
+        convolve(patches_1, base + GROUP)
         return 0
 
-    lax.fori_loop(0, OWN // 4, convolve, 0)
-
-
-def passed_along(block, distance):
-    devices = range(lax.axis_size(AXES))
-    route = [(i - distance, i) for i in devices if i - distance in devices]
-    return lax.ppermute(block, AXES, route)
+    lax.fori_loop(0, OWN // (2 * GROUP), groups, 0)
 
 
 VMEM = pl.BlockSpec(memory_space=pltpu.VMEM)
 SMEM = pl.BlockSpec(memory_space=pltpu.SMEM)
+ANY = pl.BlockSpec(memory_space=pl.ANY)
 
 
 def on_device(
     coarse_feat, coarse_children, fine_neighbours, up_weight, up_bias, conv_weight, conv_bias
 ):
-    rank = lax.axis_index(AXES)
-    children = coarse_children.reshape(-1)
-    place = jnp.where(children >= 0, children - (rank - 1) * OWN, REACH)
-    own_ids = rank * OWN + lax.broadcasted_iota(jnp.int32, (OWN, 1), 0)
-    upward = fine_neighbours[:, jnp.array(upward_columns)]
-    upward = jnp.where(upward >= 0, upward - own_ids, 0)
-    before = passed_along(upward[OWN - HALO:], 1)
-    after = passed_along(upward[:HALO], -1)
-    upward = jnp.concatenate([before, upward, after], axis=0)
-    near7 = jnp.where(upward > 0, upward + lax.broadcasted_iota(jnp.int32, (ACTIVE, 1), 0), SLOTS)
-    near26 = jnp.where(fine_neighbours >= 0, fine_neighbours - (rank * OWN - HALO), ACTIVE)
-
-    counts = (SLOTS, OWN + HALO, OWN + 2 * HALO, 2 * HALO, HALO)
-    local, up1, down1, down2, up2 = pl.pallas_call(
-        pack_kernel,
-        out_shape=[jax.ShapeDtypeStruct((count, 16, 256), BF16) for count in counts],
-        in_specs=[SMEM, VMEM],
-        out_specs=[VMEM] * 5,
-        scratch_shapes=[pltpu.VMEM((97, 16, 256), BF16), pltpu.SMEM((REACH + 8,), jnp.int32)],
-        compiler_params=pltpu.CompilerParams(vmem_limit_bytes=24 * 2 ** 20),
-        name="pack",
-    )(place, coarse_feat)
-    up1 = passed_along(up1, 1)
-    down1 = passed_along(down1, -1)
-    down2 = passed_along(down2, -2)
-    up2 = passed_along(up2, 2)
-
-    up_w, conv_w = pl.pallas_call(
-        weight_kernel,
-        out_shape=[jax.ShapeDtypeStruct((UP_K, 256), BF16), jax.ShapeDtypeStruct((CONV_K, 256), BF16)],
-        in_specs=[VMEM, VMEM],
-        out_specs=[VMEM, VMEM],
-        compiler_params=pltpu.CompilerParams(vmem_limit_bytes=24 * 2 ** 20),
-        cost_estimate=pl.CostEstimate(flops=10 ** 9, bytes_accessed=4 * 10 ** 6, transcendentals=0),
-        name="weights",
-    )(up_weight, conv_weight.T)
-
+    octs, near, up_w, conv_w = pl.pallas_call(
+        exchange_kernel,
+        out_shape=[
+            jax.ShapeDtypeStruct((SLOTS + 1, 16, 256), F32),
+            jax.ShapeDtypeStruct((OWN + 32, 26), jnp.int32),
+            jax.ShapeDtypeStruct((UP_K, 256), BF16),
+            jax.ShapeDtypeStruct((CONV_K, 256), BF16),
+        ],
+        in_specs=[SMEM, VMEM, VMEM, VMEM, VMEM],
+        out_specs=[VMEM, VMEM, ANY, ANY],
+        scratch_shapes=[
+            pltpu.VMEM((97, 16, 256), BF16),
+            pltpu.VMEM((REACH, 16, 256), BF16),
+            pltpu.VMEM((8, 128), jnp.int32),
+            pltpu.SMEM((8, 128), jnp.int32),
+            pltpu.VMEM((OWN + HALO, 16, 256), BF16),
+            pltpu.VMEM((OWN + 2 * HALO, 16, 256), BF16),
+            pltpu.VMEM((2 * HALO, 16, 256), BF16),
+            pltpu.VMEM((HALO, 16, 256), BF16),
+            pltpu.VMEM((16, 26), jnp.int32),
+            pltpu.VMEM((16, 26), jnp.int32),
+            pltpu.VMEM((UP_K, 256), BF16),
+            pltpu.VMEM((CONV_K, 256), BF16),
+            pltpu.SemaphoreType.DMA((6,)),
+            pltpu.SemaphoreType.DMA((6,)),
+            pltpu.SemaphoreType.DMA,
+            pltpu.SemaphoreType.DMA((2,)),
+        ],
+        compiler_params=pltpu.CompilerParams(
+            vmem_limit_bytes=40 * 2 ** 20, collective_id=0, has_side_effects=True),
+        name="exchange",
+    )(coarse_children, fine_neighbours, coarse_feat, up_weight, conv_weight)
     return pl.pallas_call(
         main_kernel,
         out_shape=jax.ShapeDtypeStruct((OWN, 32, 512), BF16),
-        in_specs=[SMEM, SMEM] + [VMEM] * 9,
+        in_specs=[SMEM, VMEM, ANY, VMEM, ANY, VMEM],
         out_specs=VMEM,
         scratch_shapes=[
-            pltpu.VMEM((SLOTS + 1, 16, 256), F32),
+            pltpu.VMEM((UP_K, 256), BF16),
+            pltpu.VMEM((CONV_K, 256), BF16),
             pltpu.VMEM((ACTIVE, 16, 1280), BF16),
-            pltpu.VMEM((2, ACTIVE + 1, 64, 128), F32),
-            pltpu.VMEM((4, 64, CONV_K), BF16),
+            pltpu.VMEM((2, SLOTS + 1, 64, 128), F32),
+            pltpu.VMEM((GROUP, 64, CONV_K), BF16),
+            pltpu.VMEM((GROUP, 64, CONV_K), BF16),
+            pltpu.SemaphoreType.DMA((2,)),
         ],
         compiler_params=pltpu.CompilerParams(vmem_limit_bytes=48 * 2 ** 20),
         name="convolutions",
-    )(near7.reshape(-1), near26.reshape(-1), local, up1, down1, down2, up2,
-      up_w, jnp.tile(up_bias, 8)[None, :], conv_w, jnp.tile(conv_bias, 8)[None, :])
+    )(near, octs, up_w, up_bias[None, :], conv_w, conv_bias[None, :])
 
 
 def solution(mesh):

time: 72.5 us -> 44.5 us (0.61)
  the two profiles are of different devices: /device:TPU:6 before, /device:TPU:1 now
where the time goes in v2:
time: 44.5 us; the launch traced here: 44.2 us
  Pallas kernels  38.5 us (87%)
  local copies, waits for them, and re-layouts  5.72 us (13%)
    pallas_call x1, Pallas kernels, on_device(): pl.pallas_call(exchange_kernel, out_shape=[jax.ShapeDtypeStruct((SLOTS +...  22.3 us
    pallas_call x1, Pallas kernels, on_device(): pl.pallas_call(main_kernel, out_shape=jax.ShapeDtypeStruct((OWN, 32, 512)...  16.2 us
    unnamed x12, local copies, waits for them, and re-layouts  5.72 us

profile of v2, /device:TPU:1, one launch (start us, length us, event | category | flops | bytes accessed | tf_op | source)
XLA Modules:
  0.0 44.2 jit_solution(13142743486102912408)
XLA Ops:
  0.0 0.8 %copy.8.children_ref = s32[12,8]{1,0:T(8,128)S(1)} copy(s32[12,8]{0,1:T(8,128)} %param.8) | data formatting | bytes 768 | tf_op args[1]
  0.8 0.8 %copy.9.near_ref = s32[48,26]{1,0:T(8,128)S(1)} copy(s32[48,26]{0,1:T(8,128)} %param.9) | data formatting | bytes 9984 | tf_op args[2]
  1.6 0.0 copy-start
  1.6 1.1 %copy-done = bf16[12,64,512]{2,1,0:T(8,128)(2,1)S(1)} copy-done((bf16[12,64,512]{2,1,0:T(8,128)(2,1)S(1)}, bf16[12,64,512]{2,1,0:T(8,128)(2,1)}, u32[]{:S(2)}) %copy-start) | copy-done | bytes 786456
  2.7 0.0 copy-start.1
  2.7 0.9 %copy-done.1 = bf16[64,864]{1,0:T(8,128)(2,1)S(1)} copy-done((bf16[64,864]{1,0:T(8,128)(2,1)S(1)}, bf16[64,864]{1,0:T(8,128)(2,1)}, u32[]{:S(2)}) %copy-start.1) | copy-done | bytes 110616
  3.6 0.0 copy-start.2
  3.6 0.8 %copy-done.2 = bf16[32,864]{1,0:T(8,128)(2,1)S(1)} copy-done((bf16[32,864]{1,0:T(8,128)(2,1)S(1)}, bf16[32,864]{1,0:T(8,128)(2,1)}, u32[]{:S(2)}) %copy-start.2) | copy-done | bytes 55320
  4.4 22.3 %exchange.1 = (f32[85,16,256]{2,1,0:T(8,128)S(1)}, s32[80,26]{1,0:T(8,128)S(1)}, bf16[3328,256]{1,0:T(8,128)(2,1)S(1)}, bf16[2944,256]{1,0:T(8,128)(2,1)S(1)}) custom-call(s32[12,8]{1,0:T(8,128)S(1)} %copy.8.children_ref, s32[48,26]{1,0:T(8,128)S(1)} %copy.9.near_ref, bf16[12,64,512]{2,1,0:T(8,128)(2,1)S(1)} %copy-done, bf16[64,864]{1,0:T(8,128)(2,1)S(1)} %copy-done.1, ...), custom_call_target="tpu_custom_call" | custom-call | tf_op jit(solution)/shard_map/exchange/pallas_call | solution.py:388
  26.7 0.0 copy-start.3
  26.7 0.6 %copy-done.3 = f32[32]{0:T(128)S(1)} copy-done((f32[32]{0:T(128)S(1)}, f32[32]{0:T(128)}, u32[]{:S(2)}) %copy-start.3) | copy-done | bytes 152
  27.4 0.0 copy-start.4
  27.4 0.7 %copy-done.4 = f32[32]{0:T(128)S(1)} copy-done((f32[32]{0:T(128)S(1)}, f32[32]{0:T(128)}, u32[]{:S(2)}) %copy-start.4) | copy-done | bytes 152
  28.0 16.2 %convolutions.1 = bf16[48,32,512]{2,1,0:T(8,128)(2,1)} custom-call(s32[80,26]{1,0:T(8,128)S(1)} %get-tuple-element.9.near_ref, f32[85,16,256]{2,1,0:T(8,128)S(1)} %get-tuple-element.10.octs, bf16[3328,256]{1,0:T(8,128)(2,1)S(1)} %get-tuple-element.11.up_hbm, f32[1,32]{1,0:T(1,128)S(1)} %bitcast.2, bf16[2944,256]{1,0:T(8,128)(2,1)S(1)} %get-tuple-element.12.conv_hbm, ...), custom_call_target="tpu_custom_call" | custom-call | tf_op jit(solution)/shard_map/convolutions/pallas_call | solution.py:420
Async XLA Ops:
  1.6 1.1 %copy-start = (bf16[12,64,512]{2,1,0:T(8,128)(2,1)S(1)}, bf16[12,64,512]{2,1,0:T(8,128)(2,1)}, u32[]{:S(2)}) copy-start(bf16[12,64,512]{2,1,0:T(8,128)(2,1)} %feat_ref.1) | copy-start | bytes 2359300
  2.7 0.9 %copy-start.1 = (bf16[64,864]{1,0:T(8,128)(2,1)S(1)}, bf16[64,864]{1,0:T(8,128)(2,1)}, u32[]{:S(2)}) copy-start(bf16[64,864]{1,0:T(8,128)(2,1)} %up_ref.1) | copy-start | bytes 331780
  3.6 0.8 %copy-start.2 = (bf16[32,864]{1,0:T(8,128)(2,1)S(1)}, bf16[32,864]{1,0:T(8,128)(2,1)}, u32[]{:S(2)}) copy-start(bf16[32,864]{1,0:T(8,128)(2,1)} %conv_ref.1) | copy-start | bytes 165892
  26.7 0.7 %copy-start.3 = (f32[32]{0:T(128)S(1)}, f32[32]{0:T(128)}, u32[]{:S(2)}) copy-start(f32[32]{0:T(128)} %param.11) | copy-start | bytes 388
  27.4 0.7 %copy-start.4 = (f32[32]{0:T(128)S(1)}, f32[32]{0:T(128)}, u32[]{:S(2)}) copy-start(f32[32]{0:T(128)} %param.13) | copy-start | bytes 388

commit v3 on v2

--- a/solution.py
+++ b/solution.py
@@ -13,9 +13,10 @@
 SLOTS = OWN + 3 * HALO
 ACTIVE = OWN + 2 * HALO
 REACH = 3 * OWN
-SPREAD = 4
+PACK = 3
+SPREAD = 6
 UP = 24
-GROUP = 4
+GROUP = 8
 EXTRA_AT = 9 * 256
 CONV_K = EXTRA_AT + 5 * 128
 
@@ -45,117 +46,197 @@
     return lax.broadcasted_iota(jnp.int32, shape, dim)
 
 
-def exchange_kernel(children_ref, near_ref, feat_ref, up_ref, conv_ref, octs_ref, near_out, up_hbm, conv_hbm,
-                    table, slots, source_v, source, from1, from_1, from_2, from2, near_prev, near_next,
-                    up_out, conv_out, send_sem, recv_sem, local_sem, weight_sem):
-    ranks = lax.axis_size("row") * lax.axis_size("col")
-    rank = lax.axis_index("row") * lax.axis_size("col") + lax.axis_index("col")
+def exchange_kernel(children_hbm, near_hbm, feat_hbm, up_hbm, up_b_hbm, conv_hbm, conv_b_hbm,
+                    octs_ref, near_out, up_out, conv_out, bias_out,
+                    children_ref, near_v, feat_ref, up_ref, up_b, conv_ref, conv_b,
+                    table, slots, source_v, source, from_next, from_prev, low_own, high_own, halo_next, halo_prev,
+                    near_pad, near_next, near_prev, send_sem, recv_sem, fetch_sem, feat_sem):
+    columns = lax.axis_size("col")
+    ranks = lax.axis_size("row") * columns
+    rank = lax.axis_index("row") * columns + lax.axis_index("col")
+    exists = {-1: rank > 0, 1: rank < ranks - 1}
 
     def device(offset):
         other = lax.rem(rank + offset + ranks, ranks)
-        return other // lax.axis_size("col"), lax.rem(other, lax.axis_size("col"))
+        return other // columns, lax.rem(other, columns)
 
     barrier = pltpu.get_barrier_semaphore()
-    for offset in (1, -1, 2, -2):
-        pl.semaphore_signal(barrier, inc=1, device_id=device(offset), device_id_type=pl.DeviceIdType.MESH)
-
+    for offset in (1, -1):
+        @pl.when(exists[offset])
+        def _(offset=offset):
+            pl.semaphore_signal(barrier, inc=1, device_id=device(offset), device_id_type=pl.DeviceIdType.MESH)
+
+    fetches = [pltpu.make_async_copy(src, dst, fetch_sem.at[number]) for number, (src, dst) in enumerate((
+        (children_hbm, children_ref), (near_hbm, near_v), (up_hbm, up_ref), (conv_hbm, conv_ref),
+        (up_b_hbm, up_b), (conv_b_hbm, conv_b)))]
+
+    def feat_fetch(step):
+        part = pl.ds(step * PACK, PACK)
+        return pltpu.make_async_copy(feat_hbm.at[part], feat_ref.at[part], feat_sem.at[step])
+
+    fetches[0].start()
+    for step in range(12 // PACK):
+        feat_fetch(step).start()
+    for fetch in fetches[1:]:
+        fetch.start()
+
+    fetches[0].wait()
     slot_id = iota((8, 128), 0) * 128 + iota((8, 128), 1)
     first = (rank - 1) * OWN
     chosen = jnp.full((8, 128), 96, jnp.int32)
     for c in range(12):
         for o in range(8):
-            child = children_ref[c, o]
+            child = children_ref[o, c]
             position = jnp.where(child >= 0, child - first, REACH)
             chosen = jnp.where(slot_id == position, 8 * c + o, chosen)
     source_v[...] = chosen
-    fetch = pltpu.make_async_copy(source_v, source, local_sem)
-    fetch.start()
+    source_copy = pltpu.make_async_copy(source_v, source, fetch_sem.at[6])
+    source_copy.start()
 
     low_lane = iota((64, 128), 1) < 64
     low_row = iota((8, 128), 0) < 4
     table[96] = jnp.zeros((16, 256), BF16)
 
-    def coarse_block(c, _):
-        for pair in range(2):
-            near = feat_ref[c, :, 128 * pair:128 * pair + 128].astype(F32)
-            far = feat_ref[c, :, 256 + 128 * pair:384 + 128 * pair].astype(F32)
-            top = jnp.where(low_lane, near, pltpu.roll(far, 64, 1))
-            bottom = jnp.where(low_lane, pltpu.roll(near, 64, 1), far)
-            turned = jnp.concatenate([top, bottom], axis=0).T
-            for octant in range(8):
-                ox, oy, oz = octant // 4, octant // 2 % 2, octant % 2
-                sheets = []
-                for y in range(4):
-                    at = 64 * ox + 8 * (4 * oy + y)
-                    sheets.append(turned[at:at + 8])
-                halves = []
-                for one, two in ((sheets[0], sheets[1]), (sheets[2], sheets[3])):
-                    if oz == 0:
-                        halves.append(jnp.where(low_row, one, pltpu.roll(two, 4, 0)))
-                    else:
-                        halves.append(jnp.where(low_row, pltpu.roll(one, 4, 0), two))
-                table[c * 8 + octant, :, 128 * pair:128 * pair + 128] = jnp.concatenate(
-                    halves, axis=0).astype(BF16)
+    def turn(c, pair):
+        near = feat_ref[c, :, 128 * pair:128 * pair + 128].astype(F32)
+        far = feat_ref[c, :, 256 + 128 * pair:384 + 128 * pair].astype(F32)
+        top = jnp.where(low_lane, near, pltpu.roll(far, 64, 1))
+        bottom = jnp.where(low_lane, pltpu.roll(near, 64, 1), far)
+        return jnp.concatenate([top, bottom], axis=0).T
+
+    def octants_of(turned):
+        listed = []
+        for octant in range(8):
+            ox, oy, oz = octant // 4, octant // 2 % 2, octant % 2
+            sheets = []
+            for y in range(4):
+                at = 64 * ox + 8 * (4 * oy + y)
+                sheets.append(turned[at:at + 8])
+            halves = []
+            for one, two in ((sheets[0], sheets[1]), (sheets[2], sheets[3])):
+                if oz == 0:
+                    halves.append(jnp.where(low_row, one, pltpu.roll(two, 4, 0)))
+                else:
+                    halves.append(jnp.where(low_row, pltpu.roll(one, 4, 0), two))
+            listed.append(jnp.concatenate(halves, axis=0).astype(BF16))
+        return listed
+
+    def coarse_blocks(step, _):
+        feat_fetch(step).wait()
+        turned = [[turn(step * PACK + k, pair) for pair in range(2)] for k in range(PACK)]
+        for k in range(PACK):
+            for pair in range(2):
+                for octant, value in enumerate(octants_of(turned[k][pair])):
+                    table[(step * PACK + k) * 8 + octant, :, 128 * pair:128 * pair + 128] = value
         return 0
 
-    lax.fori_loop(0, feat_ref.shape[0], coarse_block, 0)
-
-    fetch.wait()
-
-    def fill(k, _):
-        for j in range(4):
-            q = k * 4 + j
-            slots[q] = table[source[q // 128, q % 128]]
-        return 0
-
-    lax.fori_loop(0, REACH // 4, fill, 0)
-
-    pl.semaphore_wait(barrier, 4)
-    copies = []
-    for number, (src, dst, offset) in enumerate((
-            (slots.at[0:OWN + 2 * HALO], from_1, -1),
-            (slots.at[2 * OWN - HALO:REACH], from1, 1),
-            (slots.at[0:2 * HALO], from_2, -2),
-            (slots.at[REACH - HALO:REACH], from2, 2),
-            (near_ref.at[0:16], near_next, -1),
-            (near_ref.at[OWN - 16:OWN], near_prev, 1))):
-        copy = pltpu.make_async_remote_copy(
+    lax.fori_loop(0, 12 // PACK, coarse_blocks, 0)
+    source_copy.wait()
+    fetches[1].wait()
+    near_pad[...] = jnp.zeros((32, 128), jnp.int32)
+    near_pad[0:26, 0:48] = near_v[...]
+
+    def octant_at(q):
+        return table[source[q // 128, q % 128]]
+
+    def fill(start, q_start):
+        def body(k, _):
+            for j in range(8):
+                slots[start + k * 8 + j] = octant_at(q_start + k * 8 + j)
+            return 0
+        lax.fori_loop(0, OWN // 16, body, 0)
+
+    half = OWN // 2
+    plan = [
+        (slots.at[0:half], from_next.at[0:half], -1),
+        (slots.at[OWN:OWN + half], from_prev.at[0:half], 1),
+        (slots.at[half:OWN], from_next.at[half:OWN], -1),
+        (slots.at[OWN + half:2 * OWN], from_prev.at[half:OWN], 1),
+        (near_pad, near_next, -1),
+        (near_pad, near_prev, 1),
+        (low_own, halo_next, -1),
+        (high_own, halo_prev, 1),
+    ]
+
+    def transfer(number):
+        src, dst, offset = plan[number]
+        return pltpu.make_async_remote_copy(
             src_ref=src, dst_ref=dst, send_sem=send_sem.at[number], recv_sem=recv_sem.at[number],
             device_id=device(offset), device_id_type=pl.DeviceIdType.MESH)
-        copy.start()
-        copies.append(copy)
-
+
+    def send(*numbers):
+        for number in numbers:
+            @pl.when(exists[plan[number][2]])
+            def _(number=number):
+                transfer(number).start()
+
+    def sent(*numbers):
+        for number in numbers:
+            @pl.when(exists[plan[number][2]])
+            def _(number=number):
+                transfer(number).wait_send()
+
+    def landed(*numbers):
+        for number in numbers:
+            @pl.when(exists[-plan[number][2]])
+            def _(number=number):
+                transfer(number).wait_recv()
+
+    for offset, refs, near in ((1, (from_next, halo_next), near_next), (-1, (from_prev, halo_prev), near_prev)):
+        @pl.when(jnp.logical_not(exists[offset]))
+        def _(refs=refs, near=near):
+            for ref in refs:
+                ref[...] = jnp.zeros(ref.shape, BF16)
+            near[...] = jnp.full((32, 128), -1, jnp.int32)
+
+    fill(0, 0)
+    fill(OWN, 2 * OWN)
+    pl.semaphore_wait(barrier, exists[1].astype(jnp.int32) + exists[-1].astype(jnp.int32))
+    send(0, 1)
+    fill(half, half)
+    fill(OWN + half, 2 * OWN + half)
+    send(2, 3, 4, 5)
+
+    for fetch in fetches[2:]:
+        fetch.wait()
     make_weights(up_ref, conv_ref, up_out, conv_out)
-    up_copy = pltpu.make_async_copy(up_out, up_hbm, weight_sem.at[0])
-    conv_copy = pltpu.make_async_copy(conv_out, conv_hbm, weight_sem.at[1])
-    up_copy.start()
-    conv_copy.start()
-
-    def relative(value):
-        moved = value - (rank * OWN - HALO)
-        return jnp.where((value >= 0) & (moved >= 0) & (moved < SLOTS), moved, SLOTS)
-
-    near_out[16:16 + OWN] = relative(near_ref[...])
+    spread = (iota((32, 256), 0) == iota((32, 256), 1) % 32).astype(F32)
+    for number, ref in enumerate((up_b, conv_b)):
+        bias_out[8 * number:8 * number + 8] = jnp.dot(
+            jnp.broadcast_to(ref[...], (8, 32)), spread, precision=lax.Precision.HIGHEST,
+            preferred_element_type=F32)
     octs_ref[SLOTS] = jnp.zeros((16, 256), F32)
-    for copy in copies[4:] + copies[:4]:
-        copy.wait()
-    near_out[0:16] = relative(near_prev[...])
-    near_out[16 + OWN:32 + OWN] = relative(near_next[...])
-
-    def join(parts):
-        def body(u, _):
-            total = slots[u + OWN - HALO].astype(F32)
-            for ref, offset in parts:
-                total = total + ref[u - offset].astype(F32)
-            octs_ref[u] = total
+
+    def join(start, stop, copy_ref, offset):
+        def body(k, _):
+            for j in range(4):
+                b = start + k * 4 + j
+                total = octant_at(OWN + b).astype(F32) + from_next[b].astype(F32) + from_prev[b].astype(F32)
+                octs_ref[HALO + b] = total
+                if copy_ref is not None:
+                    copy_ref[b - offset] = total.astype(BF16)
             return 0
-        return body
-
-    lax.fori_loop(0, HALO, join([(from1, 0), (from2, 0)]), 0, unroll=4)
-    lax.fori_loop(HALO, OWN + HALO, join([(from1, 0), (from_1, HALO)]), 0, unroll=8)
-    lax.fori_loop(OWN + HALO, SLOTS, join([(from_1, HALO), (from_2, OWN + HALO)]), 0, unroll=4)
-    up_copy.wait()
-    conv_copy.wait()
+        lax.fori_loop(0, (stop - start) // 4, body, 0)
+
+    landed(0, 1)
+    join(0, half, low_own, 0)
+    send(6)
+    landed(2, 3)
+    join(OWN - HALO, OWN, high_own, OWN - HALO)
+    send(7)
+    join(half, OWN - HALO, None, 0)
+    landed(4, 5)
+    lane = iota((32, 128), 1)
+    near = jnp.where(lane < HALO, pltpu.roll(near_prev[...], 128 - (OWN - HALO), 1),
+                     jnp.where(lane < HALO + OWN, pltpu.roll(near_pad[...], HALO, 1),
+                               pltpu.roll(near_next[...], HALO + OWN, 1)))
+    moved = near - (rank * OWN - HALO)
+    near_out[...] = jnp.where((near >= 0) & (moved >= 0) & (moved < SLOTS), moved, SLOTS)
+    landed(7)
+    octs_ref[0:HALO] = halo_prev[...].astype(F32)
+    landed(6)
+    octs_ref[HALO + OWN:SLOTS] = halo_next[...].astype(F32)
+    sent(*range(8))
 
 
 def make_weights(up_ref, conv_ref, up_out, conv_out):
@@ -218,18 +299,7 @@
             up_out[at:at + 64] = value.astype(BF16)
 
 
-def main_kernel(near_ref, octs, up_hbm, up_b, conv_hbm, conv_b, out_ref, up_w, conv_w, shifted, hidden,
-                patches_0, patches_1, weight_sem):
-    up_copy = pltpu.make_async_copy(up_hbm, up_w, weight_sem.at[0])
-    conv_copy = pltpu.make_async_copy(conv_hbm, conv_w, weight_sem.at[1])
-    up_copy.start()
-    conv_copy.start()
-    spread = (iota((32, 256), 0) == iota((32, 256), 1) % 32).astype(F32)
-
-    def wide_bias(ref):
-        return jnp.dot(jnp.broadcast_to(ref[...], (8, 32)), spread, precision=lax.Precision.HIGHEST,
-                       preferred_element_type=F32)[0:1]
-
+def main_kernel(near_ref, octs, up_w, conv_w, bias, out_hbm, shifted, hidden, patches_0, patches_1, out_ref, out_sem):
     def shift_z(value, beyond):
         last = iota(value.shape, 0) % 4 == 3
         return jnp.where(last, pltpu.roll(beyond, 3, 0), pltpu.roll(value, 15, 0))
@@ -241,7 +311,7 @@
     low_lane16 = iota((16, 128), 1) < 64
 
     def spread_octant(h):
-        at = [near_ref[h + 4, column] for column in upward_columns]
+        at = [near_ref[column, h] for column in upward_columns]
         here, z_next, y_next, yz_next = octs[h], octs[at[0]], octs[at[1]], octs[at[2]]
         by_z = shift_z(here, z_next)
         x0, xz, xy, xyz = [octs[at[j], :, 0:128] for j in (3, 4, 5, 6)]
@@ -264,10 +334,9 @@
         return 0
 
     lax.fori_loop(0, ACTIVE // SPREAD, spread_octants, 0)
-    up_copy.wait()
 
     hidden[:, SLOTS] = jnp.zeros((2, 64, 128), F32)
-    up_bias = wide_bias(up_b)
+    up_bias = bias[0:1]
 
     def upsample(chunk, _):
         for ((py, pz), low, high, _), start in zip(CLASSES, class_starts):
@@ -284,9 +353,8 @@
         return 0
 
     lax.fori_loop(0, ACTIVE // UP, upsample, 0)
-    conv_copy.wait()
-
-    conv_bias = wide_bias(conv_b)
+
+    conv_bias = bias[8:9]
     row = iota((8, 128), 0)
     first_row, last_row = row == 0, row == 7
     low_lane8 = iota((8, 128), 1) < 64
@@ -305,7 +373,7 @@
         return jnp.concatenate([one, other], axis=0).astype(BF16)
 
     def build(patches, b, k):
-        at = {delta: near_ref[b + 16, column] for delta, column in column_of.items()}
+        at = {delta: near_ref[column, b + HALO] for delta, column in column_of.items()}
         at[(0, 0, 0)] = b + HALO
 
         def sheet(delta, y, tile):
@@ -364,6 +432,10 @@
         for k in range(GROUP):
             build(patches, base + k, k)
 
+    def write_out(step):
+        part = pl.ds(step * 2 * GROUP, 2 * GROUP)
+        return pltpu.make_async_copy(out_ref.at[part], out_hbm.at[part], out_sem.at[step])
+
     build_group(patches_0, 0)
 
     def groups(step, _):
@@ -372,68 +444,84 @@
         convolve(patches_0, base)
         build_group(patches_0, jnp.minimum(base + 2 * GROUP, OWN - GROUP))
         convolve(patches_1, base + GROUP)
+        write_out(step).start()
         return 0
 
     lax.fori_loop(0, OWN // (2 * GROUP), groups, 0)
+    for step in range(OWN // (2 * GROUP)):
+        write_out(step).wait()
 
 
 VMEM = pl.BlockSpec(memory_space=pltpu.VMEM)
 SMEM = pl.BlockSpec(memory_space=pltpu.SMEM)
-ANY = pl.BlockSpec(memory_space=pl.ANY)
+ANY = pl.BlockSpec(memory_space=pltpu.MemorySpace.HBM)
+
+
+def in_hbm(array):
+    return pltpu.with_memory_space_constraint(array, pltpu.HBM)
 
 
 def on_device(
     coarse_feat, coarse_children, fine_neighbours, up_weight, up_bias, conv_weight, conv_bias
 ):
-    octs, near, up_w, conv_w = pl.pallas_call(
+    octs, near, up_w, conv_w, bias = pl.pallas_call(
         exchange_kernel,
         out_shape=[
             jax.ShapeDtypeStruct((SLOTS + 1, 16, 256), F32),
-            jax.ShapeDtypeStruct((OWN + 32, 26), jnp.int32),
+            jax.ShapeDtypeStruct((32, 128), jnp.int32),
             jax.ShapeDtypeStruct((UP_K, 256), BF16),
             jax.ShapeDtypeStruct((CONV_K, 256), BF16),
+            jax.ShapeDtypeStruct((16, 256), F32),
         ],
-        in_specs=[SMEM, VMEM, VMEM, VMEM, VMEM],
-        out_specs=[VMEM, VMEM, ANY, ANY],
+        in_specs=[ANY] * 7,
+        out_specs=[VMEM] * 5,
         scratch_shapes=[
+            pltpu.SMEM((8, 12), jnp.int32),
+            pltpu.VMEM((26, OWN), jnp.int32),
+            pltpu.VMEM((12, 64, 512), BF16),
+            pltpu.VMEM((64, 864), BF16),
+            pltpu.VMEM((1, 32), F32),
+            pltpu.VMEM((32, 864), BF16),
+            pltpu.VMEM((1, 32), F32),
             pltpu.VMEM((97, 16, 256), BF16),
-            pltpu.VMEM((REACH, 16, 256), BF16),
+            pltpu.VMEM((2 * OWN, 16, 256), BF16),
             pltpu.VMEM((8, 128), jnp.int32),
             pltpu.SMEM((8, 128), jnp.int32),
-            pltpu.VMEM((OWN + HALO, 16, 256), BF16),
-            pltpu.VMEM((OWN + 2 * HALO, 16, 256), BF16),
+            pltpu.VMEM((OWN, 16, 256), BF16),
+            pltpu.VMEM((OWN, 16, 256), BF16),
             pltpu.VMEM((2 * HALO, 16, 256), BF16),
             pltpu.VMEM((HALO, 16, 256), BF16),
-            pltpu.VMEM((16, 26), jnp.int32),
-            pltpu.VMEM((16, 26), jnp.int32),
-            pltpu.VMEM((UP_K, 256), BF16),
-            pltpu.VMEM((CONV_K, 256), BF16),
-            pltpu.SemaphoreType.DMA((6,)),
-            pltpu.SemaphoreType.DMA((6,)),
-            pltpu.SemaphoreType.DMA,
-            pltpu.SemaphoreType.DMA((2,)),
+            pltpu.VMEM((2 * HALO, 16, 256), BF16),
+            pltpu.VMEM((HALO, 16, 256), BF16),
+            pltpu.VMEM((32, 128), jnp.int32),
+            pltpu.VMEM((32, 128), jnp.int32),
+            pltpu.VMEM((32, 128), jnp.int32),
+            pltpu.SemaphoreType.DMA((8,)),
+            pltpu.SemaphoreType.DMA((8,)),
+            pltpu.SemaphoreType.DMA((7,)),
+            pltpu.SemaphoreType.DMA((12 // PACK,)),
         ],
         compiler_params=pltpu.CompilerParams(
             vmem_limit_bytes=40 * 2 ** 20, collective_id=0, has_side_effects=True),
         name="exchange",
-    )(coarse_children, fine_neighbours, coarse_feat, up_weight, conv_weight)
+    )(*[in_hbm(x) for x in (
+        coarse_children.T, fine_neighbours.T, coarse_feat, up_weight, up_bias[None, :], conv_weight, conv_bias[None, :])])
     return pl.pallas_call(
         main_kernel,
         out_shape=jax.ShapeDtypeStruct((OWN, 32, 512), BF16),
-        in_specs=[SMEM, VMEM, ANY, VMEM, ANY, VMEM],
-        out_specs=VMEM,
+        in_specs=[SMEM, VMEM, VMEM, VMEM, VMEM],
+        out_specs=ANY,
         scratch_shapes=[
-            pltpu.VMEM((UP_K, 256), BF16),
-            pltpu.VMEM((CONV_K, 256), BF16),
             pltpu.VMEM((ACTIVE, 16, 1280), BF16),
             pltpu.VMEM((2, SLOTS + 1, 64, 128), F32),
             pltpu.VMEM((GROUP, 64, CONV_K), BF16),
             pltpu.VMEM((GROUP, 64, CONV_K), BF16),
-            pltpu.SemaphoreType.DMA((2,)),
+            pltpu.VMEM((OWN, 32, 512), BF16),
+            pltpu.SemaphoreType.DMA((OWN // (2 * GROUP),)),
         ],
         compiler_params=pltpu.CompilerParams(vmem_limit_bytes=48 * 2 ** 20),
         name="convolutions",
-    )(near, octs, up_w, up_bias[None, :], conv_w, conv_bias[None, :])
+    )(near, octs, up_w, conv_w, bias)
 
 
 def solution(mesh):

time: 44.5 us -> 34.3 us (0.77)
  the two profiles are of different devices: /device:TPU:1 before, /device:TPU:6 now
where the time goes in v3:
time: 34.3 us; the launch traced here: 34.2 us
  Pallas kernels  34.2 us (100%)
    pallas_call x1, Pallas kernels, on_device(): pl.pallas_call(exchange_kernel, out_shape=[jax.ShapeDtypeStruct((SLOTS +...  20.3 us
    pallas_call x1, Pallas kernels, on_device(): pl.pallas_call(main_kernel, out_shape=jax.ShapeDtypeStruct((OWN, 32, 512)...  13.9 us

profile of v3, /device:TPU:6, one launch (start us, length us, event | category | flops | bytes accessed | tf_op | source)
XLA Modules:
  0.0 34.2 jit_solution(14058941121348450937)
XLA Ops:
  0.0 20.3 %exchange.1 = (f32[85,16,256]{2,1,0:T(8,128)S(1)}, s32[32,128]{1,0:T(8,128)S(1)}, bf16[3328,256]{1,0:T(8,128)(2,1)S(1)}, bf16[2944,256]{1,0:T(8,128)(2,1)S(1)}, f32[16,256]{1,0:T(8,128)S(1)}) custom-call(s32[8,12]{1,0:T(8,128)} %bitcast.5, s32[26,48]{1,0:T(8,128)} %bitcast.4, bf16[12,64,512]{2,1,0:T(8,128)(2,1)} %feat_hbm.1, bf16[64,864]{1,0:T(8,128)(2,1)} %up_hbm.1, ...), custom_call_target="tpu_custom_call" | custom-call | tf_op jit(solution)/shard_map/exchange/pallas_call | solution.py:467
  20.3 13.9 %convolutions.1 = bf16[48,32,512]{2,1,0:T(8,128)(2,1)} custom-call(s32[32,128]{1,0:T(8,128)S(1)} %get-tuple-element.10.near_ref, f32[85,16,256]{2,1,0:T(8,128)S(1)} %get-tuple-element.11.octs, bf16[3328,256]{1,0:T(8,128)(2,1)S(1)} %get-tuple-element.12.up_w, bf16[2944,256]{1,0:T(8,128)(2,1)S(1)} %get-tuple-element.13.conv_w, ...), custom_call_target="tpu_custom_call" | custom-call | tf_op jit(solution)/shard_map/convolutions/pallas_call | solution.py:509

commit v4 on v3

--- a/solution.py
+++ b/solution.py
@@ -15,8 +15,8 @@
 REACH = 3 * OWN
 PACK = 3
 SPREAD = 6
-UP = 24
-GROUP = 8
+GROUP = 6
+INNER = OWN - HALO
 EXTRA_AT = 9 * 256
 CONV_K = EXTRA_AT + 5 * 128
 
@@ -47,10 +47,11 @@
 
 
 def exchange_kernel(children_hbm, near_hbm, feat_hbm, up_hbm, up_b_hbm, conv_hbm, conv_b_hbm,
-                    octs_ref, near_out, up_out, conv_out, bias_out,
+                    octs_ref, near_out, up_out, conv_out, bias_out, inner_hidden, inner_out,
                     children_ref, near_v, feat_ref, up_ref, up_b, conv_ref, conv_b,
                     table, slots, source_v, source, from_next, from_prev, low_own, high_own, halo_next, halo_prev,
-                    near_pad, near_next, near_prev, send_sem, recv_sem, fetch_sem, feat_sem):
+                    near_pad, near_next, near_prev, inner_near_v, inner_near, shifted, patches_0, patches_1,
+                    send_sem, recv_sem, fetch_sem, feat_sem):
     columns = lax.axis_size("col")
     ranks = lax.axis_size("row") * columns
     rank = lax.axis_index("row") * columns + lax.axis_index("col")
@@ -135,6 +136,12 @@
     fetches[1].wait()
     near_pad[...] = jnp.zeros((32, 128), jnp.int32)
     near_pad[0:26, 0:48] = near_v[...]
+    inside = near_pad[...] - rank * OWN
+    within = (near_pad[...] >= 0) & (inside >= 0) & (inside < OWN)
+    inner_near_v[0:32] = jnp.where(within, inside + HALO, SLOTS)
+    inner_near_v[32:64] = jnp.where(within & (inside < INNER), inside, INNER)
+    inner_copy = pltpu.make_async_copy(inner_near_v, inner_near, fetch_sem.at[7])
+    inner_copy.start()
 
     def octant_at(q):
         return table[source[q // 128, q % 128]]
@@ -206,6 +213,8 @@
             jnp.broadcast_to(ref[...], (8, 32)), spread, precision=lax.Precision.HIGHEST,
             preferred_element_type=F32)
     octs_ref[SLOTS] = jnp.zeros((16, 256), F32)
+    inner_hidden[:, INNER] = jnp.zeros((2, 64, 128), F32)
+    inner_copy.wait()
 
     def join(start, stop, copy_ref, offset):
         def body(k, _):
@@ -225,6 +234,21 @@
     join(OWN - HALO, OWN, high_own, OWN - HALO)
     send(7)
     join(half, OWN - HALO, None, 0)
+
+    spread_octants(inner_near, octs_ref, shifted, HALO, 0, INNER)
+    up_bias = bias_out[0:1]
+
+    def inner_upsample(chunk, _):
+        upsample(shifted, up_out, up_bias, inner_hidden, chunk * (INNER // 2), INNER // 2)
+        return 0
+
+    lax.fori_loop(0, 2, inner_upsample, 0)
+    build_group, convolve = convolver(
+        lambda column, b: inner_near[32 + column, b], 0, inner_hidden, conv_out, bias_out[8:9], inner_out, HALO)
+    build_group(patches_0, HALO)
+    build_group(patches_1, HALO + GROUP)
+    convolve(patches_0, HALO)
+    convolve(patches_1, HALO + GROUP)
     landed(4, 5)
     lane = iota((32, 128), 1)
     near = jnp.where(lane < HALO, pltpu.roll(near_prev[...], 128 - (OWN - HALO), 1),
@@ -299,7 +323,7 @@
             up_out[at:at + 64] = value.astype(BF16)
 
 
-def main_kernel(near_ref, octs, up_w, conv_w, bias, out_hbm, shifted, hidden, patches_0, patches_1, out_ref, out_sem):
+def spread_octants(near_ref, octs, shifted, offset, start, stop):
     def shift_z(value, beyond):
         last = iota(value.shape, 0) % 4 == 3
         return jnp.where(last, pltpu.roll(beyond, 3, 0), pltpu.roll(value, 15, 0))
@@ -312,7 +336,7 @@
 
     def spread_octant(h):
         at = [near_ref[column, h] for column in upward_columns]
-        here, z_next, y_next, yz_next = octs[h], octs[at[0]], octs[at[1]], octs[at[2]]
+        here, z_next, y_next, yz_next = octs[h + offset], octs[at[0]], octs[at[1]], octs[at[2]]
         by_z = shift_z(here, z_next)
         x0, xz, xy, xyz = [octs[at[j], :, 0:128] for j in (3, 4, 5, 6)]
         x_by_z = shift_z(x0, xz)
@@ -327,34 +351,30 @@
             (1024, shift_y(by_z, shift_z(y_next, yz_next))),
         ]
 
-    def spread_octants(group, _):
+    def group_of(group, _):
         for h, parts in [(group * SPREAD + k, spread_octant(group * SPREAD + k)) for k in range(SPREAD)]:
             for lane, value in parts:
                 shifted[h, :, lane:lane + value.shape[1]] = value.astype(BF16)
         return 0
 
-    lax.fori_loop(0, ACTIVE // SPREAD, spread_octants, 0)
-
-    hidden[:, SLOTS] = jnp.zeros((2, 64, 128), F32)
-    up_bias = bias[0:1]
-
-    def upsample(chunk, _):
-        for ((py, pz), low, high, _), start in zip(CLASSES, class_starts):
-            rows = shifted[pl.ds(chunk * UP, UP), :, low:high].reshape(16 * UP, high - low)
-            value = jnp.dot(rows, up_w[start:start + high - low], preferred_element_type=F32) + up_bias
-            half = 0.5 * value
-            value = half + half * jnp.tanh(half)
-            for b in range(UP):
-                for y in range(4):
-                    part = value[16 * b + 4 * y:16 * b + 4 * y + 4]
-                    for tile in range(2):
-                        hidden[tile, chunk * UP + b, pl.ds(8 * (2 * y + py) + pz, 4, stride=2), :] = (
-                            part[:, 128 * tile:128 * tile + 128])
-        return 0
-
-    lax.fori_loop(0, ACTIVE // UP, upsample, 0)
-
-    conv_bias = bias[8:9]
+    lax.fori_loop(start // SPREAD, stop // SPREAD, group_of, 0)
+
+
+def upsample(shifted, up_w, up_bias, hidden, start, count):
+    for ((py, pz), low, high, _), at in zip(CLASSES, class_starts):
+        rows = shifted[pl.ds(start, count), :, low:high].reshape(16 * count, high - low)
+        value = jnp.dot(rows, up_w[at:at + high - low], preferred_element_type=F32) + up_bias
+        half = 0.5 * value
+        value = half + half * jnp.tanh(half)
+        for b in range(count):
+            for y in range(4):
+                part = value[16 * b + 4 * y:16 * b + 4 * y + 4]
+                for tile in range(2):
+                    hidden[tile, start + b, pl.ds(8 * (2 * y + py) + pz, 4, stride=2), :] = (
+                        part[:, 128 * tile:128 * tile + 128])
+
+
+def convolver(nearby, offset, hidden, conv_w, conv_bias, out_ref, out_offset):
     row = iota((8, 128), 0)
     first_row, last_row = row == 0, row == 7
     low_lane8 = iota((8, 128), 1) < 64
@@ -373,8 +393,8 @@
         return jnp.concatenate([one, other], axis=0).astype(BF16)
 
     def build(patches, b, k):
-        at = {delta: near_ref[column, b + HALO] for delta, column in column_of.items()}
-        at[(0, 0, 0)] = b + HALO
+        at = {delta: nearby(column, b) for delta, column in column_of.items()}
+        at[(0, 0, 0)] = b + offset
 
         def sheet(delta, y, tile):
             return hidden[tile, at[delta], 8 * y:8 * y + 8, :]
@@ -423,32 +443,56 @@
                     one, other = turned[32 * x:32 * x + 32], turned[32 * x + 32:32 * x + 64]
                     at = 256 * half + 64 * x
                     b = base + 2 * pair
-                    out_ref[b, :, at:at + 128] = jnp.where(
+                    out_ref[b - out_offset, :, at:at + 128] = jnp.where(
                         low_lane32, one, pltpu.roll(other, 64, 1)).astype(BF16)
-                    out_ref[b + 1, :, at:at + 128] = jnp.where(
+                    out_ref[b + 1 - out_offset, :, at:at + 128] = jnp.where(
                         low_lane32, pltpu.roll(one, 64, 1), other).astype(BF16)
 
     def build_group(patches, base):
         for k in range(GROUP):
             build(patches, base + k, k)
 
+    return build_group, convolve
+
+
+def main_kernel(near_ref, octs, up_w, conv_w, bias, inner_hidden, inner_out, out_hbm,
+                shifted, hidden, patches_0, patches_1, out_ref, out_sem, inner_sem):
+    bring = pltpu.make_async_copy(inner_hidden.at[:, 0:INNER], hidden.at[:, HALO:HALO + INNER], inner_sem.at[0])
+    bring.start()
+    middle = pltpu.make_async_copy(inner_out, out_hbm.at[HALO:2 * HALO], inner_sem.at[1])
+    middle.start()
+    hidden[:, SLOTS] = jnp.zeros((2, 64, 128), F32)
+    spread_octants(near_ref, octs, shifted, 0, 0, HALO)
+    spread_octants(near_ref, octs, shifted, 0, HALO + INNER, ACTIVE)
+    up_bias = bias[0:1]
+    upsample(shifted, up_w, up_bias, hidden, 0, HALO)
+    upsample(shifted, up_w, up_bias, hidden, HALO + INNER, 2 * HALO)
+    bring.wait()
+
+    build_group, convolve = convolver(
+        lambda column, b: near_ref[column, b + HALO], HALO, hidden, conv_w, bias[8:9], out_ref, 0)
+
+    def base_of(step):
+        return jnp.where(step > 0, 2 * GROUP * (step + 1), 0)
+
     def write_out(step):
-        part = pl.ds(step * 2 * GROUP, 2 * GROUP)
+        part = pl.ds(base_of(step), 2 * GROUP)
         return pltpu.make_async_copy(out_ref.at[part], out_hbm.at[part], out_sem.at[step])
 
     build_group(patches_0, 0)
 
     def groups(step, _):
-        base = step * 2 * GROUP
+        base = base_of(step)
         build_group(patches_1, base + GROUP)
         convolve(patches_0, base)
-        build_group(patches_0, jnp.minimum(base + 2 * GROUP, OWN - GROUP))
+        build_group(patches_0, base_of(jnp.minimum(step + 1, 2)))
         convolve(patches_1, base + GROUP)
         write_out(step).start()
         return 0
 
-    lax.fori_loop(0, OWN // (2 * GROUP), groups, 0)
-    for step in range(OWN // (2 * GROUP)):
+    lax.fori_loop(0, 3, groups, 0)
+    middle.wait()
+    for step in range(3):
         write_out(step).wait()
 
 
@@ -464,7 +508,7 @@
 def on_device(
     coarse_feat, coarse_children, fine_neighbours, up_weight, up_bias, conv_weight, conv_bias
 ):
-    octs, near, up_w, conv_w, bias = pl.pallas_call(
+    octs, near, up_w, conv_w, bias, inner_hidden, inner_out = pl.pallas_call(
         exchange_kernel,
         out_shape=[
             jax.ShapeDtypeStruct((SLOTS + 1, 16, 256), F32),
@@ -472,9 +516,11 @@
             jax.ShapeDtypeStruct((UP_K, 256), BF16),
             jax.ShapeDtypeStruct((CONV_K, 256), BF16),
             jax.ShapeDtypeStruct((16, 256), F32),
+            jax.ShapeDtypeStruct((2, INNER + 1, 64, 128), F32),
+            jax.ShapeDtypeStruct((HALO, 32, 512), BF16),
         ],
         in_specs=[ANY] * 7,
-        out_specs=[VMEM] * 5,
+        out_specs=[VMEM] * 7,
         scratch_shapes=[
             pltpu.SMEM((8, 12), jnp.int32),
             pltpu.VMEM((26, OWN), jnp.int32),
@@ -496,20 +542,25 @@
             pltpu.VMEM((32, 128), jnp.int32),
             pltpu.VMEM((32, 128), jnp.int32),
             pltpu.VMEM((32, 128), jnp.int32),
+            pltpu.VMEM((64, 128), jnp.int32),
+            pltpu.SMEM((64, 128), jnp.int32),
+            pltpu.VMEM((INNER, 16, 1280), BF16),
+            pltpu.VMEM((GROUP, 64, CONV_K), BF16),
+            pltpu.VMEM((GROUP, 64, CONV_K), BF16),
             pltpu.SemaphoreType.DMA((8,)),
             pltpu.SemaphoreType.DMA((8,)),
-            pltpu.SemaphoreType.DMA((7,)),
+            pltpu.SemaphoreType.DMA((8,)),
             pltpu.SemaphoreType.DMA((12 // PACK,)),
         ],
         compiler_params=pltpu.CompilerParams(
-            vmem_limit_bytes=40 * 2 ** 20, collective_id=0, has_side_effects=True),
+            vmem_limit_bytes=32 * 2 ** 20, collective_id=0, has_side_effects=True),
         name="exchange",
     )(*[in_hbm(x) for x in (
         coarse_children.T, fine_neighbours.T, coarse_feat, up_weight, up_bias[None, :], conv_weight, conv_bias[None, :])])
     return pl.pallas_call(
         main_kernel,
         out_shape=jax.ShapeDtypeStruct((OWN, 32, 512), BF16),
-        in_specs=[SMEM, VMEM, VMEM, VMEM, VMEM],
+        in_specs=[SMEM] + [VMEM] * 6,
         out_specs=ANY,
         scratch_shapes=[
             pltpu.VMEM((ACTIVE, 16, 1280), BF16),
@@ -517,11 +568,12 @@
             pltpu.VMEM((GROUP, 64, CONV_K), BF16),
             pltpu.VMEM((GROUP, 64, CONV_K), BF16),
             pltpu.VMEM((OWN, 32, 512), BF16),
-            pltpu.SemaphoreType.DMA((OWN // (2 * GROUP),)),
+            pltpu.SemaphoreType.DMA((3,)),
+            pltpu.SemaphoreType.DMA((2,)),
         ],
-        compiler_params=pltpu.CompilerParams(vmem_limit_bytes=48 * 2 ** 20),
+        compiler_params=pltpu.CompilerParams(vmem_limit_bytes=28 * 2 ** 20),
         name="convolutions",
-    )(near, octs, up_w, conv_w, bias)
+    )(near, octs, up_w, conv_w, bias, inner_hidden, inner_out)
 
 
 def solution(mesh):

time: 34.3 us -> 30.5 us (0.89)
  Pallas kernels: 34.2 us -> 30.3 us
    pallas_call x1, Pallas kernels: 13.9 us -> 10 us  [on_device(): pl.pallas_call(main_kernel, out_shape=jax.ShapeDtypeStruct((OWN, 32, 512)...]
where the time goes in v4:
time: 30.5 us; the launch traced here: 30.4 us
  Pallas kernels  30.3 us (99%)
    pallas_call x1, Pallas kernels, on_device(): pl.pallas_call(exchange_kernel, out_shape=[jax.ShapeDtypeStruct((SLOTS +...  20.3 us
    pallas_call x1, Pallas kernels, on_device(): pl.pallas_call(main_kernel, out_shape=jax.ShapeDtypeStruct((OWN, 32, 512)...  10 us

profile of v4, /device:TPU:6, one launch (start us, length us, event | category | flops | bytes accessed | tf_op | source)
XLA Modules:
  0.0 30.4 jit_solution(2642307653523171847)
XLA Ops:
  0.0 20.3 %exchange.1 = (f32[85,16,256]{2,1,0:T(8,128)S(1)}, s32[32,128]{1,0:T(8,128)S(1)}, bf16[3328,256]{1,0:T(8,128)(2,1)S(1)}, bf16[2944,256]{1,0:T(8,128)(2,1)S(1)}, ...) custom-call(s32[8,12]{1,0:T(8,128)} %bitcast.5, s32[26,48]{1,0:T(8,128)} %bitcast.4, ...), custom_call_target="tpu_custom_call" | custom-call | tf_op jit(solution)/shard_map/exchange/pallas_call | solution.py:511
  20.3 10.0 %convolutions.1 = bf16[48,32,512]{2,1,0:T(8,128)(2,1)} custom-call(s32[32,128]{1,0:T(8,128)S(1)} %get-tuple-element.12.near_ref, f32[85,16,256]{2,1,0:T(8,128)S(1)} %get-tuple-element.13.octs, bf16[3328,256]{1,0:T(8,128)(2,1)S(1)} %get-tuple-element.14.up_w, bf16[2944,256]{1,0:T(8,128)(2,1)S(1)} %get-tuple-element.15.conv_w, ...), custom_call_target="tpu_custom_call" | custom-call | tf_op jit(solution)/shard_map/convolutions/pallas_call | solution.py:560

commit v5 on v4

--- a/solution.py
+++ b/solution.py
@@ -13,7 +13,7 @@
 SLOTS = OWN + 3 * HALO
 ACTIVE = OWN + 2 * HALO
 REACH = 3 * OWN
-PACK = 3
+PACK = 6
 SPREAD = 6
 GROUP = 6
 INNER = OWN - HALO
@@ -28,18 +28,19 @@
 upward_columns = [column_of[delta] for delta in upward_list]
 
 CLASSES = [
-    ((0, 0), 256, 1024 - 256, {(0, 0): (1, 1)}),
-    ((0, 1), 256, 1024, {(0, 0): (1, 2), (0, 1): (1, 0)}),
-    ((1, 0), 0, 768, {(0, 0): (2, 1), (1, 0): (0, 1)}),
-    ((1, 1), 0, 1280, {(0, 0): (2, 2), (0, 1): (2, 0), (1, 0): (0, 2), (1, 1): (0, 0)}),
+    ((0, 0), 256, 512, {(0, 0): (1, 1)}),
+    ((0, 1), 256, 768, {(0, 0): (1, 2), (0, 1): (1, 0)}),
+    ((1, 0), 0, 512, {(0, 0): (2, 1), (1, 0): (0, 1)}),
+    ((1, 1), 0, 1024, {(0, 0): (2, 2), (0, 1): (2, 0), (1, 0): (0, 2), (1, 1): (0, 0)}),
 ]
-SHIFT_AT = {(1, 0): 0, (0, 0): 512, (0, 1): 768, (1, 1): 1024}
-HALO_AT = 256
+SHIFT_AT = {(1, 0): 0, (0, 0): 256, (0, 1): 512, (1, 1): 768}
+HALO_AT = 1024
 class_starts = []
-UP_K = 0
+UP_MAIN = 0
 for _, low, high, _ in CLASSES:
-    class_starts.append(UP_K)
-    UP_K += high - low
+    class_starts.append(UP_MAIN)
+    UP_MAIN += high - low
+UP_K = UP_MAIN + 256
 
 
 def iota(shape, dim):
@@ -49,7 +50,7 @@
 def exchange_kernel(children_hbm, near_hbm, feat_hbm, up_hbm, up_b_hbm, conv_hbm, conv_b_hbm,
                     octs_ref, near_out, up_out, conv_out, bias_out, inner_hidden, inner_out,
                     children_ref, near_v, feat_ref, up_ref, up_b, conv_ref, conv_b,
-                    table, slots, source_v, source, from_next, from_prev, low_own, high_own, halo_next, halo_prev,
+                    table, slots, source_v, source, from_next, from_prev, low_own, edge_own, high_own, halo_next, edge_next, halo_prev,
                     near_pad, near_next, near_prev, inner_near_v, inner_near, shifted, patches_0, patches_1,
                     send_sem, recv_sem, fetch_sem, feat_sem):
     columns = lax.axis_size("col")
@@ -163,6 +164,7 @@
         (near_pad, near_prev, 1),
         (low_own, halo_next, -1),
         (high_own, halo_prev, 1),
+        (edge_own, edge_next, -1),
     ]
 
     def transfer(number):
@@ -189,7 +191,7 @@
             def _(number=number):
                 transfer(number).wait_recv()
 
-    for offset, refs, near in ((1, (from_next, halo_next), near_next), (-1, (from_prev, halo_prev), near_prev)):
+    for offset, refs, near in ((1, (from_next, halo_next, edge_next), near_next), (-1, (from_prev, halo_prev), near_prev)):
         @pl.when(jnp.logical_not(exists[offset]))
         def _(refs=refs, near=near):
             for ref in refs:
@@ -227,9 +229,24 @@
             return 0
         lax.fori_loop(0, (stop - start) // 4, body, 0)
 
+    sub = iota((8, 128), 0)
+
+    def join_low(k, _):
+        for j in range(2):
+            edges = []
+            for b in (k * 4 + 2 * j, k * 4 + 2 * j + 1):
+                total = octant_at(OWN + b).astype(F32) + from_next[b].astype(F32) + from_prev[b].astype(F32)
+                octs_ref[HALO + b] = total
+                low_own[b] = total[:, 0:128].astype(BF16)
+                first, second = total[0:8, 128:256], total[8:16, 128:256]
+                edges.append(jnp.where(sub < 5, first, jnp.where(
+                    sub == 5, pltpu.roll(second, 5, 0), pltpu.roll(second, 2, 0))))
+            edge_own[k * 2 + j] = jnp.concatenate(edges, axis=0).astype(BF16)
+        return 0
+
     landed(0, 1)
-    join(0, half, low_own, 0)
-    send(6)
+    lax.fori_loop(0, half // 4, join_low, 0)
+    send(6, 8)
     landed(2, 3)
     join(OWN - HALO, OWN, high_own, OWN - HALO)
     send(7)
@@ -258,9 +275,20 @@
     near_out[...] = jnp.where((near >= 0) & (moved >= 0) & (moved < SLOTS), moved, SLOTS)
     landed(7)
     octs_ref[0:HALO] = halo_prev[...].astype(F32)
-    landed(6)
-    octs_ref[HALO + OWN:SLOTS] = halo_next[...].astype(F32)
-    sent(*range(8))
+    landed(6, 8)
+
+    def spread_low(k, _):
+        edges = edge_next[k].astype(F32)
+        for j in range(2):
+            u = HALO + OWN + 2 * k + j
+            octs_ref[u, :, 0:128] = halo_next[2 * k + j].astype(F32)
+            edge = edges[8 * j:8 * j + 8]
+            octs_ref[u, 0:8, 128:256] = edge
+            octs_ref[u, 8:16, 128:256] = jnp.where(sub == 0, pltpu.roll(edge, 3, 0), pltpu.roll(edge, 6, 0))
+        return 0
+
+    lax.fori_loop(0, HALO, spread_low, 0)
+    sent(*range(9))
 
 
 def make_weights(up_ref, conv_ref, up_out, conv_out):
@@ -315,12 +343,14 @@
                 for kx in range(3):
                     value = jnp.where(lane_f == 2 * x + kx - 1, taps[kx], value)
                 up_out[at + 64 * x:at + 64 * x + 64] = value.astype(BF16)
-        for number, shift in enumerate(((0, 0), (0, 1), (1, 0), (1, 1))):
-            at = start + HALO_AT - low + 64 * number
-            value = zero_up
+    for number, shift in enumerate(((0, 0), (0, 1), (1, 0), (1, 1))):
+        value = zero_up
+        for k, (_, _, _, taps_of) in enumerate(CLASSES):
             if shift in taps_of:
-                value = jnp.where(lane_f == 7, up_tap(0, *taps_of[shift]), zero_up)
-            up_out[at:at + 64] = value.astype(BF16)
+                group = 4 * (k % 2) + (3 if k < 2 else 2)
+                value = jnp.where(lane_f == group, up_tap(0, *taps_of[shift]), value)
+        at = UP_MAIN + 64 * number
+        up_out[at:at + 64] = value.astype(BF16)
 
 
 def spread_octants(near_ref, octs, shifted, offset, start, stop):
@@ -344,11 +374,11 @@
         x_by_yz = shift_y(x_by_z, shift_z(xy, xyz))
         return [
             (0, shift_y(here, y_next)),
-            (256, jnp.where(low_lane16, x0, pltpu.roll(x_by_z, 64, 1))),
-            (384, jnp.where(low_lane16, x_by_y, pltpu.roll(x_by_yz, 64, 1))),
-            (512, here),
-            (768, by_z),
-            (1024, shift_y(by_z, shift_z(y_next, yz_next))),
+            (256, here),
+            (512, by_z),
+            (768, shift_y(by_z, shift_z(y_next, yz_next))),
+            (1024, jnp.where(low_lane16, x0, pltpu.roll(x_by_z, 64, 1))),
+            (1152, jnp.where(low_lane16, x_by_y, pltpu.roll(x_by_yz, 64, 1))),
         ]
 
     def group_of(group, _):
@@ -361,17 +391,25 @@
 
 
 def upsample(shifted, up_w, up_bias, hidden, start, count):
-    for ((py, pz), low, high, _), at in zip(CLASSES, class_starts):
+    def product(low, high, at):
         rows = shifted[pl.ds(start, count), :, low:high].reshape(16 * count, high - low)
-        value = jnp.dot(rows, up_w[at:at + high - low], preferred_element_type=F32) + up_bias
-        half = 0.5 * value
-        value = half + half * jnp.tanh(half)
-        for b in range(count):
-            for y in range(4):
-                part = value[16 * b + 4 * y:16 * b + 4 * y + 4]
-                for tile in range(2):
+        return jnp.dot(rows, up_w[at:at + high - low], preferred_element_type=F32)
+
+    halo = product(HALO_AT, HALO_AT + 256, UP_MAIN)
+    reached = iota((16 * count, 128), 1) >= 96
+    for k, (((py, pz), low, high, _), at) in enumerate(zip(CLASSES, class_starts)):
+        beyond = halo[:, 128 * (k % 2):128 * (k % 2) + 128]
+        if k >= 2:
+            beyond = pltpu.roll(beyond, 32, 1)
+        value = product(low, high, at) + up_bias
+        tiles = [value[:, 0:128], value[:, 128:256] + jnp.where(reached, beyond, 0.0)]
+        for tile in range(2):
+            half = 0.5 * tiles[tile]
+            value = half + half * jnp.tanh(half)
+            for b in range(count):
+                for y in range(4):
                     hidden[tile, start + b, pl.ds(8 * (2 * y + py) + pz, 4, stride=2), :] = (
-                        part[:, 128 * tile:128 * tile + 128])
+                        value[16 * b + 4 * y:16 * b + 4 * y + 4])
 
 
 def convolver(nearby, offset, hidden, conv_w, conv_bias, out_ref, out_offset):
@@ -535,9 +573,11 @@
             pltpu.SMEM((8, 128), jnp.int32),
             pltpu.VMEM((OWN, 16, 256), BF16),
             pltpu.VMEM((OWN, 16, 256), BF16),
-            pltpu.VMEM((2 * HALO, 16, 256), BF16),
+            pltpu.VMEM((2 * HALO, 16, 128), BF16),
+            pltpu.VMEM((HALO, 16, 128), BF16),
             pltpu.VMEM((HALO, 16, 256), BF16),
-            pltpu.VMEM((2 * HALO, 16, 256), BF16),
+            pltpu.VMEM((2 * HALO, 16, 128), BF16),
+            pltpu.VMEM((HALO, 16, 128), BF16),
             pltpu.VMEM((HALO, 16, 256), BF16),
             pltpu.VMEM((32, 128), jnp.int32),
             pltpu.VMEM((32, 128), jnp.int32),
@@ -547,8 +587,8 @@
             pltpu.VMEM((INNER, 16, 1280), BF16),
             pltpu.VMEM((GROUP, 64, CONV_K), BF16),
             pltpu.VMEM((GROUP, 64, CONV_K), BF16),
-            pltpu.SemaphoreType.DMA((8,)),
-            pltpu.SemaphoreType.DMA((8,)),
+            pltpu.SemaphoreType.DMA((9,)),
+            pltpu.SemaphoreType.DMA((9,)),
             pltpu.SemaphoreType.DMA((8,)),
             pltpu.SemaphoreType.DMA((12 // PACK,)),
         ],

time: 30.5 us -> 30.3 us (level)
  no operation moved by 1% of the time
where the time goes in v5:
time: 30.3 us; the launch traced here: 30.2 us
  Pallas kernels  30.2 us (100%)
    pallas_call x1, Pallas kernels, on_device(): pl.pallas_call(exchange_kernel, out_shape=[jax.ShapeDtypeStruct((SLOTS +...  20.4 us
    pallas_call x1, Pallas kernels, on_device(): pl.pallas_call(main_kernel, out_shape=jax.ShapeDtypeStruct((OWN, 32, 512)...  9.84 us

profile of v5, /device:TPU:6, one launch (start us, length us, event | category | flops | bytes accessed | tf_op | source)
XLA Modules:
  0.0 30.2 jit_solution(12901573903343750555)
XLA Ops:
  0.0 20.4 %exchange.1 = (f32[85,16,256]{2,1,0:T(8,128)S(1)}, s32[32,128]{1,0:T(8,128)S(1)}, bf16[2560,256]{1,0:T(8,128)(2,1)S(1)}, bf16[2944,256]{1,0:T(8,128)(2,1)S(1)}, ...) custom-call(s32[8,12]{1,0:T(8,128)} %bitcast.5, s32[26,48]{1,0:T(8,128)} %bitcast.4, ...), custom_call_target="tpu_custom_call" | custom-call | tf_op jit(solution)/shard_map/exchange/pallas_call | solution.py:549
  20.4 9.8 %convolutions.1 = bf16[48,32,512]{2,1,0:T(8,128)(2,1)} custom-call(s32[32,128]{1,0:T(8,128)S(1)} %get-tuple-element.12.near_ref, f32[85,16,256]{2,1,0:T(8,128)S(1)} %get-tuple-element.13.octs, bf16[2560,256]{1,0:T(8,128)(2,1)S(1)} %get-tuple-element.14.up_w, bf16[2944,256]{1,0:T(8,128)(2,1)S(1)} %get-tuple-element.15.conv_w, ...), custom_call_target="tpu_custom_call" | custom-call | tf_op jit(solution)/shard_map/convolutions/pallas_call | solution.py:600

commit v6 on v5

--- a/solution.py
+++ b/solution.py
@@ -51,7 +51,7 @@
                     octs_ref, near_out, up_out, conv_out, bias_out, inner_hidden, inner_out,
                     children_ref, near_v, feat_ref, up_ref, up_b, conv_ref, conv_b,
                     table, slots, source_v, source, from_next, from_prev, low_own, edge_own, high_own, halo_next, edge_next, halo_prev,
-                    near_pad, near_next, near_prev, inner_near_v, inner_near, shifted, patches_0, patches_1,
+                    near_pad, near_next, near_prev, inner_near_v, inner_near, all_near, shifted, patches_0, patches_1,
                     send_sem, recv_sem, fetch_sem, feat_sem):
     columns = lax.axis_size("col")
     ranks = lax.axis_size("row") * columns
@@ -138,9 +138,9 @@
     near_pad[...] = jnp.zeros((32, 128), jnp.int32)
     near_pad[0:26, 0:48] = near_v[...]
     inside = near_pad[...] - rank * OWN
-    within = (near_pad[...] >= 0) & (inside >= 0) & (inside < OWN)
+    within = (near_pad[...] >= 0) & (inside >= 0) & (inside < OWN + HALO)
     inner_near_v[0:32] = jnp.where(within, inside + HALO, SLOTS)
-    inner_near_v[32:64] = jnp.where(within & (inside < INNER), inside, INNER)
+    inner_near_v[32:64] = jnp.where(within, inside + HALO, ACTIVE)
     inner_copy = pltpu.make_async_copy(inner_near_v, inner_near, fetch_sem.at[7])
     inner_copy.start()
 
@@ -215,7 +215,7 @@
             jnp.broadcast_to(ref[...], (8, 32)), spread, precision=lax.Precision.HIGHEST,
             preferred_element_type=F32)
     octs_ref[SLOTS] = jnp.zeros((16, 256), F32)
-    inner_hidden[:, INNER] = jnp.zeros((2, 64, 128), F32)
+    inner_hidden[:, ACTIVE] = jnp.zeros((2, 64, 128), F32)
     inner_copy.wait()
 
     def join(start, stop, copy_ref, offset):
@@ -252,20 +252,6 @@
     send(7)
     join(half, OWN - HALO, None, 0)
 
-    spread_octants(inner_near, octs_ref, shifted, HALO, 0, INNER)
-    up_bias = bias_out[0:1]
-
-    def inner_upsample(chunk, _):
-        upsample(shifted, up_out, up_bias, inner_hidden, chunk * (INNER // 2), INNER // 2)
-        return 0
-
-    lax.fori_loop(0, 2, inner_upsample, 0)
-    build_group, convolve = convolver(
-        lambda column, b: inner_near[32 + column, b], 0, inner_hidden, conv_out, bias_out[8:9], inner_out, HALO)
-    build_group(patches_0, HALO)
-    build_group(patches_1, HALO + GROUP)
-    convolve(patches_0, HALO)
-    convolve(patches_1, HALO + GROUP)
     landed(4, 5)
     lane = iota((32, 128), 1)
     near = jnp.where(lane < HALO, pltpu.roll(near_prev[...], 128 - (OWN - HALO), 1),
@@ -273,8 +259,31 @@
                                pltpu.roll(near_next[...], HALO + OWN, 1)))
     moved = near - (rank * OWN - HALO)
     near_out[...] = jnp.where((near >= 0) & (moved >= 0) & (moved < SLOTS), moved, SLOTS)
-    landed(7)
-    octs_ref[0:HALO] = halo_prev[...].astype(F32)
+    near_copy = pltpu.make_async_copy(near_out, all_near, fetch_sem.at[8])
+    near_copy.start()
+
+    spread_octants(inner_near, octs_ref, shifted, HALO, 0, INNER)
+    up_bias = bias_out[0:1]
+
+    def inner_upsample(chunk, _):
+        upsample(shifted, up_out, up_bias, inner_hidden, chunk * (INNER // 2), INNER // 2, HALO)
+        return 0
+
+    lax.fori_loop(0, 2, inner_upsample, 0)
+    build_group, convolve = convolver(
+        lambda column, b: inner_near[32 + column, b], HALO, inner_hidden, conv_out, bias_out[8:9], inner_out, HALO)
+
+    def middle_groups(step, _):
+        base = HALO + 2 * GROUP * step
+        build_group(patches_0, base)
+        build_group(patches_1, base + GROUP)
+        convolve(patches_0, base)
+        convolve(patches_1, base + GROUP)
+        return 0
+
+    lax.fori_loop(0, 1, middle_groups, 0)
+
+    near_copy.wait()
     landed(6, 8)
 
     def spread_low(k, _):
@@ -288,6 +297,12 @@
         return 0
 
     lax.fori_loop(0, HALO, spread_low, 0)
+    spread_octants(all_near, octs_ref, shifted, 0, HALO + INNER, ACTIVE)
+    upsample(shifted, up_out, up_bias, inner_hidden, HALO + INNER, 2 * HALO)
+    lax.fori_loop(1, 3, middle_groups, 0)
+
+    landed(7)
+    octs_ref[0:HALO] = halo_prev[...].astype(F32)
     sent(*range(9))
 
 
@@ -390,7 +405,7 @@
     lax.fori_loop(start // SPREAD, stop // SPREAD, group_of, 0)
 
 
-def upsample(shifted, up_w, up_bias, hidden, start, count):
+def upsample(shifted, up_w, up_bias, hidden, start, count, offset=0):
     def product(low, high, at):
         rows = shifted[pl.ds(start, count), :, low:high].reshape(16 * count, high - low)
         return jnp.dot(rows, up_w[at:at + high - low], preferred_element_type=F32)
@@ -408,7 +423,7 @@
             value = half + half * jnp.tanh(half)
             for b in range(count):
                 for y in range(4):
-                    hidden[tile, start + b, pl.ds(8 * (2 * y + py) + pz, 4, stride=2), :] = (
+                    hidden[tile, start + b + offset, pl.ds(8 * (2 * y + py) + pz, 4, stride=2), :] = (
                         value[16 * b + 4 * y:16 * b + 4 * y + 4])
 
 
@@ -495,43 +510,29 @@
 
 def main_kernel(near_ref, octs, up_w, conv_w, bias, inner_hidden, inner_out, out_hbm,
                 shifted, hidden, patches_0, patches_1, out_ref, out_sem, inner_sem):
-    bring = pltpu.make_async_copy(inner_hidden.at[:, 0:INNER], hidden.at[:, HALO:HALO + INNER], inner_sem.at[0])
+    known = pl.ds(HALO, 2 * HALO)
+    bring = pltpu.make_async_copy(inner_hidden.at[:, known], hidden.at[:, known], inner_sem.at[0])
     bring.start()
-    middle = pltpu.make_async_copy(inner_out, out_hbm.at[HALO:2 * HALO], inner_sem.at[1])
-    middle.start()
+    done = pltpu.make_async_copy(inner_out, out_hbm.at[HALO:OWN], inner_sem.at[1])
+    done.start()
     hidden[:, SLOTS] = jnp.zeros((2, 64, 128), F32)
     spread_octants(near_ref, octs, shifted, 0, 0, HALO)
-    spread_octants(near_ref, octs, shifted, 0, HALO + INNER, ACTIVE)
-    up_bias = bias[0:1]
-    upsample(shifted, up_w, up_bias, hidden, 0, HALO)
-    upsample(shifted, up_w, up_bias, hidden, HALO + INNER, 2 * HALO)
+    upsample(shifted, up_w, bias[0:1], hidden, 0, HALO)
     bring.wait()
 
     build_group, convolve = convolver(
         lambda column, b: near_ref[column, b + HALO], HALO, hidden, conv_w, bias[8:9], out_ref, 0)
-
-    def base_of(step):
-        return jnp.where(step > 0, 2 * GROUP * (step + 1), 0)
-
-    def write_out(step):
-        part = pl.ds(base_of(step), 2 * GROUP)
-        return pltpu.make_async_copy(out_ref.at[part], out_hbm.at[part], out_sem.at[step])
-
+    writes = []
     build_group(patches_0, 0)
-
-    def groups(step, _):
-        base = base_of(step)
-        build_group(patches_1, base + GROUP)
-        convolve(patches_0, base)
-        build_group(patches_0, base_of(jnp.minimum(step + 1, 2)))
-        convolve(patches_1, base + GROUP)
-        write_out(step).start()
-        return 0
-
-    lax.fori_loop(0, 3, groups, 0)
-    middle.wait()
-    for step in range(3):
-        write_out(step).wait()
+    build_group(patches_1, GROUP)
+    for number, patches in enumerate((patches_0, patches_1)):
+        convolve(patches, number * GROUP)
+        part = pl.ds(number * GROUP, GROUP)
+        write = pltpu.make_async_copy(out_ref.at[part], out_hbm.at[part], out_sem.at[number])
+        write.start()
+        writes.append(write)
+    for copy in [done] + writes:
+        copy.wait()
 
 
 VMEM = pl.BlockSpec(memory_space=pltpu.VMEM)
@@ -554,8 +555,8 @@
             jax.ShapeDtypeStruct((UP_K, 256), BF16),
             jax.ShapeDtypeStruct((CONV_K, 256), BF16),
             jax.ShapeDtypeStruct((16, 256), F32),
-            jax.ShapeDtypeStruct((2, INNER + 1, 64, 128), F32),
-            jax.ShapeDtypeStruct((HALO, 32, 512), BF16),
+            jax.ShapeDtypeStruct((2, ACTIVE + 1, 64, 128), F32),
+            jax.ShapeDtypeStruct((INNER, 32, 512), BF16),
         ],
         in_specs=[ANY] * 7,
         out_specs=[VMEM] * 7,
@@ -584,12 +585,13 @@
             pltpu.VMEM((32, 128), jnp.int32),
             pltpu.VMEM((64, 128), jnp.int32),
             pltpu.SMEM((64, 128), jnp.int32),
-            pltpu.VMEM((INNER, 16, 1280), BF16),
+            pltpu.SMEM((32, 128), jnp.int32),
+            pltpu.VMEM((ACTIVE, 16, 1280), BF16),
             pltpu.VMEM((GROUP, 64, CONV_K), BF16),
             pltpu.VMEM((GROUP, 64, CONV_K), BF16),
             pltpu.SemaphoreType.DMA((9,)),
             pltpu.SemaphoreType.DMA((9,)),
-            pltpu.SemaphoreType.DMA((8,)),
+            pltpu.SemaphoreType.DMA((9,)),
             pltpu.SemaphoreType.DMA((12 // PACK,)),
         ],
         compiler_params=pltpu.CompilerParams(
@@ -607,8 +609,8 @@
             pltpu.VMEM((2, SLOTS + 1, 64, 128), F32),
             pltpu.VMEM((GROUP, 64, CONV_K), BF16),
             pltpu.VMEM((GROUP, 64, CONV_K), BF16),
-            pltpu.VMEM((OWN, 32, 512), BF16),
-            pltpu.SemaphoreType.DMA((3,)),
+            pltpu.VMEM((HALO, 32, 512), BF16),
+            pltpu.SemaphoreType.DMA((2,)),
             pltpu.SemaphoreType.DMA((2,)),
         ],
         compiler_params=pltpu.CompilerParams(vmem_limit_bytes=28 * 2 ** 20),

time: 30.3 us -> 28.9 us (0.954)
  Pallas kernels: 30.2 us -> 28.8 us
    pallas_call x1, Pallas kernels: 9.84 us -> 4.51 us  [on_device(): pl.pallas_call(main_kernel, out_shape=jax.ShapeDtypeStruct((OWN, 32, 512)...]
    pallas_call x1, Pallas kernels: 20.4 us -> 24.3 us  [on_device(): pl.pallas_call(exchange_kernel, out_shape=[jax.ShapeDtypeStruct((SLOTS +...]
where the time goes in v6:
time: 28.9 us; the launch traced here: 28.8 us
  Pallas kernels  28.8 us (100%)
    pallas_call x1, Pallas kernels, on_device(): pl.pallas_call(exchange_kernel, out_shape=[jax.ShapeDtypeStruct((SLOTS +...  24.3 us
    pallas_call x1, Pallas kernels, on_device(): pl.pallas_call(main_kernel, out_shape=jax.ShapeDtypeStruct((OWN, 32, 512)...  4.51 us

profile of v6, /device:TPU:6, one launch (start us, length us, event | category | flops | bytes accessed | tf_op | source)
XLA Modules:
  0.0 28.8 jit_solution(7646085931214690019)
XLA Ops:
  0.0 24.3 %exchange.1 = (f32[85,16,256]{2,1,0:T(8,128)S(1)}, s32[32,128]{1,0:T(8,128)S(1)}, bf16[2560,256]{1,0:T(8,128)(2,1)S(1)}, bf16[2944,256]{1,0:T(8,128)(2,1)S(1)}, ...) custom-call(s32[8,12]{1,0:T(8,128)} %bitcast.5, s32[26,48]{1,0:T(8,128)} %bitcast.4, ...), custom_call_target="tpu_custom_call" | custom-call | tf_op jit(solution)/shard_map/exchange/pallas_call | solution.py:550
  24.3 4.5 %convolutions.1 = bf16[48,32,512]{2,1,0:T(8,128)(2,1)} custom-call(s32[32,128]{1,0:T(8,128)S(1)} %get-tuple-element.12.near_ref, f32[85,16,256]{2,1,0:T(8,128)S(1)} %get-tuple-element.13.octs, bf16[2560,256]{1,0:T(8,128)(2,1)S(1)} %get-tuple-element.14.up_w, bf16[2944,256]{1,0:T(8,128)(2,1)S(1)} %get-tuple-element.15.conv_w, ...), custom_call_target="tpu_custom_call" | custom-call | tf_op jit(solution)/shard_map/convolutions/pallas_call | solution.py:602

commit v7 on v6

--- a/solution.py
+++ b/solution.py
@@ -247,6 +247,10 @@
     landed(0, 1)
     lax.fori_loop(0, half // 4, join_low, 0)
     send(6, 8)
+
+    up_bias = bias_out[0:1]
+    spread_octants(inner_near, octs_ref, shifted, HALO, 0, HALO)
+    upsample(shifted, up_out, up_bias, inner_hidden, 0, HALO, HALO)
     landed(2, 3)
     join(OWN - HALO, OWN, high_own, OWN - HALO)
     send(7)
@@ -262,14 +266,8 @@
     near_copy = pltpu.make_async_copy(near_out, all_near, fetch_sem.at[8])
     near_copy.start()
 
-    spread_octants(inner_near, octs_ref, shifted, HALO, 0, INNER)
-    up_bias = bias_out[0:1]
-
-    def inner_upsample(chunk, _):
-        upsample(shifted, up_out, up_bias, inner_hidden, chunk * (INNER // 2), INNER // 2, HALO)
-        return 0
-
-    lax.fori_loop(0, 2, inner_upsample, 0)
+    spread_octants(inner_near, octs_ref, shifted, HALO, HALO, INNER)
+    upsample(shifted, up_out, up_bias, inner_hidden, HALO, INNER - HALO, HALO)
     build_group, convolve = convolver(
         lambda column, b: inner_near[32 + column, b], HALO, inner_hidden, conv_out, bias_out[8:9], inner_out, HALO)
 

time: 28.9 us -> 28.5 us (0.986)
  Pallas kernels: 28.8 us -> 28.4 us
    pallas_call x1, Pallas kernels: 24.3 us -> 23.9 us  [on_device(): pl.pallas_call(exchange_kernel, out_shape=[jax.ShapeDtypeStruct((SLOTS +...]
where the time goes in v7:
time: 28.5 us; the launch traced here: 28.4 us
  Pallas kernels  28.4 us (100%)
    pallas_call x1, Pallas kernels, on_device(): pl.pallas_call(exchange_kernel, out_shape=[jax.ShapeDtypeStruct((SLOTS +...  23.9 us
    pallas_call x1, Pallas kernels, on_device(): pl.pallas_call(main_kernel, out_shape=jax.ShapeDtypeStruct((OWN, 32, 512)...  4.51 us

profile of v7, /device:TPU:6, one launch (start us, length us, event | category | flops | bytes accessed | tf_op | source)
XLA Modules:
  0.0 28.4 jit_solution(15489232059169024130)
XLA Ops:
  0.0 23.9 %exchange.1 = (f32[85,16,256]{2,1,0:T(8,128)S(1)}, s32[32,128]{1,0:T(8,128)S(1)}, bf16[2560,256]{1,0:T(8,128)(2,1)S(1)}, bf16[2944,256]{1,0:T(8,128)(2,1)S(1)}, ...) custom-call(s32[8,12]{1,0:T(8,128)} %bitcast.5, s32[26,48]{1,0:T(8,128)} %bitcast.4, ...), custom_call_target="tpu_custom_call" | custom-call | tf_op jit(solution)/shard_map/exchange/pallas_call | solution.py:548
  23.9 4.5 %convolutions.1 = bf16[48,32,512]{2,1,0:T(8,128)(2,1)} custom-call(s32[32,128]{1,0:T(8,128)S(1)} %get-tuple-element.12.near_ref, f32[85,16,256]{2,1,0:T(8,128)S(1)} %get-tuple-element.13.octs, bf16[2560,256]{1,0:T(8,128)(2,1)S(1)} %get-tuple-element.14.up_w, bf16[2944,256]{1,0:T(8,128)(2,1)S(1)} %get-tuple-element.15.conv_w, ...), custom_call_target="tpu_custom_call" | custom-call | tf_op jit(solution)/shard_map/convolutions/pallas_call | solution.py:600
